TPU v7x, 128 devices: a whole 4x4x4 slice. The times are simulated.
128 devices in a mesh: row: 8 (over y_lo, z), col: 16 (over x, y_hi, core).
Axes of the slice: x: 4, y: 4 (y_hi: 2, y_lo: 2; y = y_hi * 2 + y_lo), z: 4, core: 2. Of those that a mesh axis runs over, the one named last changes fastest.
Arguments:
- x_blocks: bfloat16 [2048, 2048, 128], P('row', 'col'), may hold values from -0.046875 to 0.046875
- block_ids: int32 [2048, 16], P('row', 'col'), may hold values from 0 to 511, as said below
- margins: float32 [32768], P('row'), may hold values from -6 to 6
- deleted: int32 [4096], P('row'), may hold values from 0 to 32767, as said below
- grads: float32 [32768, 128], P('col'), may hold values from -6 to 6
Outputs:
- solution: float32 [32768, 128], P('col')
- residual: float32 [32768, 128], P('col')
Inputs may be any that keep to these rules, and one draw needn't show every extreme that they name: `block_ids`: each device's 256 entries are distinct and rise; each device lists the first and the last block of its grid. `deleted`: the 512 entries of row shard r are distinct rows of that shard, r * 4096 and up; each shard deletes its first and its last row.
All inputs are finite; a program needn't handle non-finite values.
Results may differ from a plain program's by a relative error of at most 0.015.
Values may be sent and summed in bfloat16 or wider, within the bound.
A program may use at most 128 MiB of HBM per device.

v0:
```python
import jax
import jax.numpy as jnp
from jax import lax
from jax.sharding import Mesh
from jax.sharding import PartitionSpec as P

ITERS = 3
ROW = ("row_0", "row_1")
COL = ("col_0", "col_1", "col_2")
ROW_COL = ("row_0", "row_1", "col_0", "col_1", "col_2")


highest = lax.Precision.HIGHEST
ridge_weight = 0.2


def cut_along(shard, dim, size):
    before, after = (shard.shape[:dim], shard.shape[dim + 1 :])
    return jnp.moveaxis(shard.reshape(*before, size, -1, *after), dim, 0)


def sent_and_summed(shard, axis, dim):
    pieces = cut_along(shard, dim, lax.axis_size(axis))
    arrived = lax.all_to_all(pieces, axis, split_axis=0, concat_axis=0, tiled=True)
    return arrived.sum(axis=0)


def from_everyone(shard, axis):
    size = lax.axis_size(axis)
    return lax.all_to_all(
        jnp.broadcast_to(shard[None], (size, *shard.shape)), axis, 0, 0, tiled=True
    )


def laid_out(pieces, dim):
    shape = list(pieces.shape[1:])
    shape[dim] *= pieces.shape[0]
    return jnp.moveaxis(pieces, 0, dim).reshape(shape)


def gather_directly(shard, axis, dim):
    pieces = from_everyone(shard, axis)
    return laid_out(pieces, dim)


def by_axis(shard, axes):
    for axis in axes:
        shard = lax.psum(shard, axis)
    return shard


def in_one_piece(arrays, axis, dim, along):
    both = jnp.concatenate(arrays, axis=along)
    result, at, outs = (lax.all_gather(both, axis, axis=dim, tiled=True), 0, [])
    for a in arrays:
        outs.append(lax.slice_in_dim(result, at, at + a.shape[along], axis=along))
        at += a.shape[along]
    return tuple(outs)


def on_device(x_blocks, block_ids, margins, deleted, grads):
    block_width = x_blocks.shape[1]
    feature_rows = grads.shape[0]
    directions = grads.shape[1]
    row_count = margins.shape[0]
    row_blocks = row_count // block_width
    feature_blocks = feature_rows // block_width
    pattern = block_ids[:, 0]
    block_row = pattern // feature_blocks
    block_column = pattern % feature_blocks
    row_select = (block_row[:, None] == jnp.arange(row_blocks, dtype=jnp.int32)[None, :]).astype(
        jnp.float32
    )
    column_select = (
        block_column[:, None] == jnp.arange(feature_blocks, dtype=jnp.int32)[None, :]
    ).astype(jnp.float32)
    global_rows = lax.axis_index(ROW) * row_count + jnp.arange(row_count, dtype=jnp.int32)
    removed = jnp.any(global_rows[:, None] == deleted[None, :], axis=1)
    logistic = jax.nn.sigmoid(margins)
    weights_flat = jnp.where(removed, 0.0, logistic * (1.0 - logistic))
    row_share_count = row_count // lax.axis_size(COL)
    row_offset = lax.axis_index(COL) * row_share_count
    share_rows = feature_rows // lax.axis_size(ROW)
    offset = lax.axis_index(ROW) * share_rows
    residual = lax.dynamic_slice_in_dim(grads, offset, share_rows, 0)
    solution = jnp.zeros_like(residual)
    direction = residual
    mine = residual
    norm_now = by_axis(jnp.sum(mine * mine, axis=0), ROW_COL)
    for iteration in range(ITERS):
        apply_rounded = direction.astype(jnp.bfloat16)
        gathered = gather_directly(apply_rounded, ROW, 0)
        picked_tiles = gathered.reshape(feature_blocks, block_width, directions)[block_column]
        forward = jnp.einsum(
            "bij,bjk->bik", x_blocks, picked_tiles, preferred_element_type=jnp.float32
        )
        partial_rows = jnp.einsum("br,bik->rik", row_select, forward, precision=highest)
        flat_rows = partial_rows.reshape(row_count, directions)
        own_sum = sent_and_summed(flat_rows, COL, 0)
        own_weights = lax.dynamic_slice_in_dim(weights_flat, row_offset, row_share_count, 0)
        own_scaled = (own_weights[:, None] * own_sum).astype(jnp.bfloat16)
        scaled = gather_directly(own_scaled, COL, 0).reshape(row_blocks, block_width, directions)
        picked_rows = scaled[block_row]
        backward = jnp.einsum(
            "bji,bjk->bik", x_blocks, picked_rows, preferred_element_type=jnp.float32
        )
        summed = jnp.einsum("bc,bik->cik", column_select, backward, precision=highest)
        hessian_image = (
            sent_and_summed(summed.reshape(feature_rows, directions), ROW, 0)
            + ridge_weight * direction
        )
        own_residual = residual
        curvature, cross_term, image_square = (
            by_axis(jnp.sum(direction * hessian_image, axis=0), ROW_COL),
            by_axis(jnp.sum(own_residual * hessian_image, axis=0), ROW_COL),
            by_axis(jnp.sum(hessian_image * hessian_image, axis=0), ROW_COL),
        )
        step_size = norm_now / curvature
        norm_next = norm_now - 2.0 * step_size * cross_term + step_size * step_size * image_square
        solution = solution + step_size * direction
        residual = residual - step_size * hessian_image
        if iteration + 1 < ITERS:
            direction = residual + norm_next / norm_now * direction
            norm_now = norm_next
    solution, residual = tuple(
        (
            part.astype(jnp.float32)
            for part in in_one_piece(
                (solution.astype(jnp.bfloat16), residual.astype(jnp.bfloat16)), ROW, 0, 1
            )
        )
    )
    return (solution, residual)


def solution(mesh):
    torus = Mesh(mesh.devices.reshape(2, 4, 4, 2, 2), ("row_0", "row_1", "col_0", "col_1", "col_2"))
    in_specs = (P(ROW, COL, None), P(ROW, COL), P(ROW), P(ROW), P(COL, None))
    out_specs = (P(COL, None), P(COL, None))
    return jax.shard_map(
        on_device, mesh=torus, in_specs=in_specs, out_specs=out_specs, check_vma=False
    )
```

profile of v0, /device:TPU:0, one launch (start us, length us, event | category | flops | bytes accessed | tf_op | source)
XLA Modules:
  0.0 715.4 jit_solution(13770284594476689411)
XLA Ops:
  16.1 8.9 %all-to-all-done = bf16[8,256,128]{2,1,0:T(8,128)(2,1)S(1)} async-done(((bf16[8,256,128]{2,1,0:T(8,128)(2,1)}), bf16[8,256,128]{2,1,0:T(8,128)(2,1)S(1)}, u32[]{:S(2)}, u32[]{:S(2)}) %all-to-all-start) | async-done | bytes 524320 | tf_op jit(solution)/shard_map/all_to_all | solution.py:30
  33.5 12.8 %convolution_bitcast_fusion.5 = f32[256,128,128]{1,2,0:T(8,128)} fusion(bf16[256,128,128]{2,1,0:T(8,128)(2,1)} %gather_fusion, bf16[256,128,128]{2,1,0:T(8,128)(2,1)} %param.5), kind=kOutput, calls=%fused_computation.11 | convolution fusion | flops 1073741824 | bytes 33554432 | tf_op jit(solution)/shard_map/bij,bjk->bik/dot_general | solution.py:94
  46.4 17.5 %copy.26 = f32[256,128,128]{2,0,1:T(8,128)} copy(f32[256,128,128]{1,2,0:T(8,128)} %convolution_bitcast_fusion.5) | data formatting | bytes 33554432 | tf_op jit(solution)/shard_map/bij,bjk->bik/dot_general | solution.py:94
  63.8 9.7 %fusion.5 = f32[32,128,128]{2,0,1:T(8,128)S(1)} fusion(f32[256,128,128]{2,0,1:T(8,128)} %copy.26, s32[256]{0:T(256)S(1)} %bitcast.71), kind=kOutput, calls=%fused_computation.40 | convolution fusion | flops 1610620928 | bytes 18875392 | tf_op jit(solution)/shard_map/br,bik->rik/dot_general | solution.py:97
  84.6 27.5 %all-to-all-done.1 = f32[16,256,128]{2,1,0:T(8,128)S(1)} async-done(((f32[16,256,128]{2,1,0:T(8,128)}), f32[16,256,128]{2,1,0:T(8,128)S(1)}, u32[]{:S(2)}, u32[]{:S(2)}) %all-to-all-start.1) | async-done | bytes 2097184 | tf_op jit(solution)/shard_map/all_to_all | solution.py:24
  118.7 17.7 %all-to-all-done.2 = bf16[16,256,128]{2,1,0:T(8,128)(2,1)S(1)} async-done(((bf16[16,256,128]{2,1,0:T(8,128)(2,1)}), bf16[16,256,128]{2,1,0:T(8,128)(2,1)S(1)}, u32[]{:S(2)}, u32[]{:S(2)}) %all-to-all-start.2) | async-done | bytes 1048608 | tf_op jit(solution)/shard_map/all_to_all | solution.py:30
  145.1 14.4 %convolution_bitcast_fusion.4 = f32[256,128,128]{1,2,0:T(8,128)} fusion(bf16[256,128,128]{2,1,0:T(8,128)(2,1)} %gather_fusion.1, bf16[256,128,128]{2,1,0:T(8,128)(2,1)} %param.5), kind=kOutput, calls=%fused_computation.10 | convolution fusion | flops 1073741824 | bytes 33554432 | tf_op jit(solution)/shard_map/bji,bjk->bik/dot_general | solution.py:104
  159.4 17.5 %copy.29 = f32[256,128,128]{2,0,1:T(8,128)} copy(f32[256,128,128]{1,2,0:T(8,128)} %convolution_bitcast_fusion.4) | data formatting | bytes 33554432 | tf_op jit(solution)/shard_map/bji,bjk->bik/dot_general | solution.py:104
  176.9 9.0 %fusion.15 = f32[16,128,128]{2,0,1:T(8,128)S(1)} fusion(f32[256,128,128]{2,0,1:T(8,128)} %copy.29, s32[256]{0:T(256)S(1)} %bitcast.68), kind=kOutput, calls=%fused_computation.49 | convolution fusion | flops 805310464 | bytes 17826816 | tf_op jit(solution)/shard_map/bc,bik->cik/dot_general | solution.py:107
  186.3 18.3 %all_to_all.60 = f32[8,256,128]{2,1,0:T(8,128)S(1)} all-to-all(f32[8,256,128]{2,1,0:T(8,128)S(1)} %bitcast.65), channel_id=1, replica_groups=mesh['row_0'=2,'row_1'=4,'col_0'=4,'col_1'=2,'col_2'=2] {'row_0','row_1'}, dimensions={0} | all-to-all | bytes 2097152 | tf_op jit(solution)/shard_map/all_to_all | solution.py:24
  237.6 13.4 %all_to_all.61 = bf16[8,256,128]{2,1,0:T(8,128)(2,1)S(1)} all-to-all(bf16[8,256,128]{2,1,0:T(8,128)(2,1)S(1)} %broadcast_in_dim.19), channel_id=1, replica_groups=mesh['row_0'=2,'row_1'=4,'col_0'=4,'col_1'=2,'col_2'=2] {'row_0','row_1'}, dimensions={0} | all-to-all | bytes 1048576 | tf_op jit(solution)/shard_map/all_to_all | solution.py:30
  259.6 12.8 %convolution_bitcast_fusion.3 = f32[256,128,128]{1,2,0:T(8,128)} fusion(bf16[256,128,128]{2,1,0:T(8,128)(2,1)} %gather_fusion.2, bf16[256,128,128]{2,1,0:T(8,128)(2,1)} %param.5), kind=kOutput, calls=%fused_computation.9 | convolution fusion | flops 1073741824 | bytes 33554432 | tf_op jit(solution)/shard_map/bij,bjk->bik/dot_general | solution.py:94
  272.4 17.5 %copy.32 = f32[256,128,128]{2,0,1:T(8,128)} copy(f32[256,128,128]{1,2,0:T(8,128)} %convolution_bitcast_fusion.3) | data formatting | bytes 33554432 | tf_op jit(solution)/shard_map/bij,bjk->bik/dot_general | solution.py:94
  289.9 9.7 %fusion.3 = f32[32,128,128]{2,0,1:T(8,128)S(1)} fusion(f32[256,128,128]{2,0,1:T(8,128)} %copy.32, s32[256]{0:T(256)S(1)} %bitcast.72), kind=kOutput, calls=%fused_computation.39 | convolution fusion | flops 1610620928 | bytes 18875392 | tf_op jit(solution)/shard_map/br,bik->rik/dot_general | solution.py:97
  300.9 32.3 %all_to_all.62 = f32[16,256,128]{2,1,0:T(8,128)S(1)} all-to-all(f32[16,256,128]{2,1,0:T(8,128)S(1)} %bitcast.63), channel_id=1, replica_groups=mesh['row_0'=2,'row_1'=4,'col_0'=4,'col_1'=2,'col_2'=2] {'col_0','col_1'..., dimensions={0} | all-to-all | bytes 4194304 | tf_op jit(solution)/shard_map/all_to_all | solution.py:24
  333.6 20.8 %all_to_all.63 = bf16[16,256,128]{2,1,0:T(8,128)(2,1)S(1)} all-to-all(bf16[16,256,128]{2,1,0:T(8,128)(2,1)S(1)} %broadcast_in_dim.20), channel_id=1, replica_groups=mesh['row_0'=2,'row_1'=4,'col_0'=4,'col_1'=2,'col_2'=2] {'col_0','col_1'..., dimensions={0} | all-to-all | bytes 2097152 | tf_op jit(solution)/shard_map/all_to_all | solution.py:30
  363.0 14.4 %convolution_bitcast_fusion.2 = f32[256,128,128]{1,2,0:T(8,128)} fusion(bf16[256,128,128]{2,1,0:T(8,128)(2,1)} %gather_fusion.3, bf16[256,128,128]{2,1,0:T(8,128)(2,1)} %param.5), kind=kOutput, calls=%fused_computation.8 | convolution fusion | flops 1073741824 | bytes 33554432 | tf_op jit(solution)/shard_map/bji,bjk->bik/dot_general | solution.py:104
  377.3 17.5 %copy.35 = f32[256,128,128]{2,0,1:T(8,128)} copy(f32[256,128,128]{1,2,0:T(8,128)} %convolution_bitcast_fusion.2) | data formatting | bytes 33554432 | tf_op jit(solution)/shard_map/bji,bjk->bik/dot_general | solution.py:104
  394.8 9.0 %fusion.13 = f32[16,128,128]{2,0,1:T(8,128)S(1)} fusion(f32[256,128,128]{2,0,1:T(8,128)} %copy.35, s32[256]{0:T(256)S(1)} %bitcast.69), kind=kOutput, calls=%fused_computation.48 | convolution fusion | flops 805310464 | bytes 17826816 | tf_op jit(solution)/shard_map/bc,bik->cik/dot_general | solution.py:107
  404.2 17.7 %all_to_all.64 = f32[8,256,128]{2,1,0:T(8,128)S(1)} all-to-all(f32[8,256,128]{2,1,0:T(8,128)S(1)} %bitcast.66), channel_id=1, replica_groups=mesh['row_0'=2,'row_1'=4,'col_0'=4,'col_1'=2,'col_2'=2] {'row_0','row_1'}, dimensions={0} | all-to-all | bytes 2097152 | tf_op jit(solution)/shard_map/all_to_all | solution.py:24
  435.5 8.8 %all-reduce = (f32[128]{0:T(128)S(1)}, f32[128]{0:T(128)S(1)}, f32[128]{0:T(128)S(1)}) all-reduce(f32[128]{0:T(128)S(1)} %get-tuple-element.14, f32[128]{0:T(128)S(1)} %get-tuple-element.15, f32[128]{0:T(128)S(1)} %get-tuple-element.16), channel_id=1, replica_groups=mesh['row_0'=2,'row_1'=4,'col_0'=4,'col_1'=2,'col_2'=2] {'col_0'}, use_global_device_ids=true, to_apply=%region_38.39 | all-reduce | flops 384 | bytes 3072 | tf_op jit(solution)/shard_map/psum | solution.py:48
  453.3 13.2 %all_to_all.65 = bf16[8,256,128]{2,1,0:T(8,128)(2,1)S(1)} all-to-all(bf16[8,256,128]{2,1,0:T(8,128)(2,1)S(1)} %broadcast_in_dim.21), channel_id=1, replica_groups=mesh['row_0'=2,'row_1'=4,'col_0'=4,'col_1'=2,'col_2'=2] {'row_0','row_1'}, dimensions={0} | all-to-all | bytes 1048576 | tf_op jit(solution)/shard_map/all_to_all | solution.py:30
  475.1 12.8 %convolution_bitcast_fusion.1 = f32[256,128,128]{1,2,0:T(8,128)} fusion(bf16[256,128,128]{2,1,0:T(8,128)(2,1)} %gather_fusion.4, bf16[256,128,128]{2,1,0:T(8,128)(2,1)} %param.5), kind=kOutput, calls=%fused_computation.7 | convolution fusion | flops 1073741824 | bytes 33554432 | tf_op jit(solution)/shard_map/bij,bjk->bik/dot_general | solution.py:94
  487.9 17.5 %copy.38 = f32[256,128,128]{2,0,1:T(8,128)} copy(f32[256,128,128]{1,2,0:T(8,128)} %convolution_bitcast_fusion.1) | data formatting | bytes 33554432 | tf_op jit(solution)/shard_map/bij,bjk->bik/dot_general | solution.py:94
  505.4 9.8 %fusion.1 = f32[32,128,128]{2,0,1:T(8,128)S(1)} fusion(f32[256,128,128]{2,0,1:T(8,128)} %copy.38, s32[256]{0:T(256)S(1)} %bitcast.73), kind=kOutput, calls=%fused_computation.38 | convolution fusion | flops 1610620928 | bytes 18875392 | tf_op jit(solution)/shard_map/br,bik->rik/dot_general | solution.py:97
  516.4 32.4 %all_to_all.66 = f32[16,256,128]{2,1,0:T(8,128)S(1)} all-to-all(f32[16,256,128]{2,1,0:T(8,128)S(1)} %bitcast.64), channel_id=1, replica_groups=mesh['row_0'=2,'row_1'=4,'col_0'=4,'col_1'=2,'col_2'=2] {'col_0','col_1'..., dimensions={0} | all-to-all | bytes 4194304 | tf_op jit(solution)/shard_map/all_to_all | solution.py:24
  549.2 20.8 %all_to_all.67 = bf16[16,256,128]{2,1,0:T(8,128)(2,1)S(1)} all-to-all(bf16[16,256,128]{2,1,0:T(8,128)(2,1)S(1)} %broadcast_in_dim.22), channel_id=1, replica_groups=mesh['row_0'=2,'row_1'=4,'col_0'=4,'col_1'=2,'col_2'=2] {'col_0','col_1'..., dimensions={0} | all-to-all | bytes 2097152 | tf_op jit(solution)/shard_map/all_to_all | solution.py:30
  578.7 14.4 %convolution_bitcast_fusion = f32[256,128,128]{1,2,0:T(8,128)} fusion(bf16[256,128,128]{2,1,0:T(8,128)(2,1)} %gather_fusion.5, bf16[256,128,128]{2,1,0:T(8,128)(2,1)} %param.5), kind=kOutput, calls=%fused_computation.6 | convolution fusion | flops 1073741824 | bytes 33554432 | tf_op jit(solution)/shard_map/bji,bjk->bik/dot_general | solution.py:104
  593.1 17.5 %copy.41 = f32[256,128,128]{2,0,1:T(8,128)} copy(f32[256,128,128]{1,2,0:T(8,128)} %convolution_bitcast_fusion) | data formatting | bytes 33554432 | tf_op jit(solution)/shard_map/bji,bjk->bik/dot_general | solution.py:104
  610.5 9.0 %fusion.11 = f32[16,128,128]{2,0,1:T(8,128)S(1)} fusion(f32[256,128,128]{2,0,1:T(8,128)} %copy.41, s32[256]{0:T(256)S(1)} %bitcast.70), kind=kOutput, calls=%fused_computation.47 | convolution fusion | flops 805310464 | bytes 17826816 | tf_op jit(solution)/shard_map/bc,bik->cik/dot_general | solution.py:107
  619.9 17.7 %all_to_all.68 = f32[8,256,128]{2,1,0:T(8,128)S(1)} all-to-all(f32[8,256,128]{2,1,0:T(8,128)S(1)} %bitcast.67), channel_id=1, replica_groups=mesh['row_0'=2,'row_1'=4,'col_0'=4,'col_1'=2,'col_2'=2] {'row_0','row_1'}, dimensions={0} | all-to-all | bytes 2097152 | tf_op jit(solution)/shard_map/all_to_all | solution.py:24
  670.5 35.0 %all-gather.2.cloned.1.call-done = bf16[2048,256]{1,0:T(8,128)(2,1)} async-done(((bf16[256,256]{1,0:T(8,128)(2,1)}), bf16[2048,256]{1,0:T(8,128)(2,1)}) %all-gather.2.cloned.1.call-update) | async-done | bytes 1048592 | tf_op jit(solution)/shard_map/all_gather | solution.py:54
  (70 shorter events, 173.4 us)
Async XLA Ops:
  9.0 16.0 %all-to-all-start = ((bf16[8,256,128]{2,1,0:T(8,128)(2,1)}), bf16[8,256,128]{2,1,0:T(8,128)(2,1)S(1)}, u32[]{:S(2)}, u32[]{:S(2)}) async-start(bf16[8,256,128]{2,1,0:T(8,128)(2,1)} %broadcast_in_dim.17), calls=%async_computation | async-start | bytes 1048576 | tf_op jit(solution)/shard_map/all_to_all | solution.py:30
  73.6 9.4 %copy-start = (f32[4096]{0:T(1024)S(1)}, f32[4096]{0:T(1024)}, u32[]{:S(2)}) copy-start(f32[4096]{0:T(1024)} %param.7) | copy-start | bytes 49156
  73.6 9.4 %copy-start.1 = (s32[512]{0:T(512)S(1)}, s32[512]{0:T(512)}, u32[]{:S(2)}) copy-start(s32[512]{0:T(512)} %param.8) | copy-start | bytes 6148
  76.2 36.0 %all-to-all-start.1 = ((f32[16,256,128]{2,1,0:T(8,128)}), f32[16,256,128]{2,1,0:T(8,128)S(1)}, u32[]{:S(2)}, u32[]{:S(2)}) async-start(f32[16,256,128]{2,1,0:T(8,128)} %bitcast.62), calls=%async_computation.1 | async-start | bytes 4194304 | tf_op jit(solution)/shard_map/all_to_all | solution.py:24
  113.6 22.9 %all-to-all-start.2 = ((bf16[16,256,128]{2,1,0:T(8,128)(2,1)}), bf16[16,256,128]{2,1,0:T(8,128)(2,1)S(1)}, u32[]{:S(2)}, u32[]{:S(2)}) async-start(bf16[16,256,128]{2,1,0:T(8,128)(2,1)} %broadcast_in_dim.18), calls=%async_computation.2 | async-start | bytes 2097152 | tf_op jit(solution)/shard_map/all_to_all | solution.py:30
  118.5 587.1 %all-gather.2.cloned.1.call-start = ((), (), s32[]{:S(2)}) async-start(), calls=%async_computation.12 | async-start | bytes 1179648 | tf_op jit(solution)/shard_map/all_gather | solution.py:54
Sparse Core Ops, SparseCore 0:
  670.6 34.8 all-gather.1
where the time goes:
time: 726 us; the launch traced here: 715 us
  blocking collectives  280 us (39%)
  local copies, waits for them, and re-layouts  166 us (23%)
  matrix products  138 us (19%)
  waiting for transfers between devices  89.1 us (12%)
  starting transfers between devices  18.3 us (3%)
  between operations  14.7 us (2%)
  other arithmetic  9.51 us (1%)
    all_to_all x5, blocking collectives, sent_and_summed(): lax.all_to_all(pieces, axis, split_axis=0, concat_axis=0, tiled=True)  118 us
    psum x15, blocking collectives, by_axis(): shard = lax.psum(shard, axis)  93.2 us
    all_to_all x4, blocking collectives, from_everyone(): lax.all_to_all(jnp.broadcast_to(shard[None], (size, *shard.shape)), axis,...  68.2 us
    dot_general x3, local copies, waits for them, and re-layouts, on_device(): jnp.einsum('bij,bjk->bik', x_blocks, picked_tiles, preferred_element_type...  52.4 us
    dot_general x3, local copies, waits for them, and re-layouts, on_device(): jnp.einsum('bji,bjk->bik', x_blocks, picked_rows, preferred_element_type=...  52.4 us
    dot_general x3, matrix products, on_device(): jnp.einsum('bji,bjk->bik', x_blocks, picked_rows, preferred_element_type=...  43.1 us
    dot_general x3, matrix products, on_device(): jnp.einsum('bij,bjk->bik', x_blocks, picked_tiles, preferred_element_type...  38.5 us
    all_gather x1, waiting for transfers between devices, in_one_piece(): result, at, outs = (lax.all_gather(both, axis, axis=dim, tiled=True), 0, [])  35 us
  transfers between devices with their start and end apart: 4, of which 4 were waited for; matrix products, arithmetic and copies ran while one was open for 0% of the time, Pallas kernels for 0%

commit v1 on v0

v1 whole, which is shorter than its diff:
```python
import functools

import jax
import jax.numpy as jnp
from jax import lax
from jax.experimental import pallas as pl
from jax.experimental.pallas import tpu as pltpu
from jax.sharding import PartitionSpec as P

ITERS = 3
RIDGE = 0.2
N_ROW, N_COL, N_CHIP = 8, 16, 8
BLK, DIRS, FB, RB, NBLK = 128, 128, 16, 32, 256
PIECE = 256
f32, bf16 = jnp.float32, jnp.bfloat16
MESH = pl.DeviceIdType.MESH


def tile(x, table, j, p, across):
    at = lambda a, b: x[table[(2 * j + a) * FB + 2 * p + b]]
    if across:
        top = jnp.concatenate([at(0, 0), at(1, 0)], axis=1)
        low = jnp.concatenate([at(0, 1), at(1, 1)], axis=1)
    else:
        top = jnp.concatenate([at(0, 0), at(0, 1)], axis=1)
        low = jnp.concatenate([at(1, 0), at(1, 1)], axis=1)
    return jnp.concatenate([top, low], axis=0)


def dot(a, b):
    return jnp.dot(a, b, preferred_element_type=f32)


def total(product):
    return jnp.sum((product[:, :BLK] + product[:, BLK:]).T, axis=0, keepdims=True)


def spread(row):
    square = jnp.broadcast_to(row, (DIRS, DIRS)).T
    return jnp.concatenate([square, square], axis=1)


def kernel(
    table, weights, grads, x_hbm, sol, res,
    x, xt, d, v, psend, prec, pown, csend, crec, s, acc, isend, irec, u,
    sc1, sc2, rr, coef,
    xsem, ps, pr, cs, cr, fs, fr, ss, sr, ims, imr, us, ur, s1s, s1r, s2s, s2r,
):
    r, c = lax.axis_index("row"), lax.axis_index("col")
    q, k = c // 2, c % 2
    sibling = (r, q * 2 + 1 - k)

    def chip(o):
        return ((q // 2 + o // 2) % 4) * 2 + (q % 2 + o % 2) % 2

    def chip_from(o):
        return ((q // 2 + 4 - o // 2) % 4) * 2 + (q % 2 + o % 2) % 2

    def rowdev(o):
        return ((r // 4 + o // 4) % 2) * 4 + (r % 4 + o % 4) % 4

    def rowdev_from(o):
        return ((r // 4 + o // 4) % 2) * 4 + (r % 4 + 4 - o % 4) % 4

    def remote(src, dst, send, recv, to):
        return pltpu.make_async_remote_copy(
            src_ref=src, dst_ref=dst, send_sem=send, recv_sem=recv, device_id=to, device_id_type=MESH
        )

    barrier = pltpu.get_barrier_semaphore()
    for o in range(1, N_ROW):
        pl.semaphore_signal(barrier, inc=1, device_id=(rowdev(o), c), device_id_type=MESH)
    for o in range(1, N_COL):
        pl.semaphore_signal(barrier, inc=1, device_id=(r, (c + o) % N_COL), device_id_type=MESH)

    parts = 8
    size = NBLK // parts
    loads = [
        pltpu.make_async_copy(x_hbm.at[pl.ds(i * size, size)], x.at[pl.ds(i * size, size)], xsem.at[i])
        for i in range(parts)
    ]
    for load in loads:
        load.start()
    x[NBLK] = jnp.zeros((BLK, BLK), bf16)
    xt[NBLK] = jnp.zeros((BLK, BLK), bf16)

    norm = jnp.zeros((DIRS, PIECE), f32)
    for p in range(N_ROW):
        piece = grads[p]
        d[p] = piece
        v[p] = piece.astype(bf16)
        res[p] = piece
        sol[p] = jnp.zeros((DIRS, PIECE), f32)
    mine = grads[r]
    rr[...] = jnp.broadcast_to(total(mine * mine), (8, DIRS))
    for i in range(parts):
        loads[i].wait()

        def turn(b, _, i=i):
            xt[i * size + b] = x[i * size + b].T
            return 0

        lax.fori_loop(0, size, turn, 0, unroll=4)

    pl.semaphore_wait(barrier, N_ROW - 1 + N_COL - 1)

    def iteration(t, _):
        def forward(j):
            out = dot(v[0], tile(xt, table, j, 0, True))
            for p in range(1, N_ROW):
                out += dot(v[p], tile(xt, table, j, p, True))
            return out

        def to_sibling(o):
            return remote(psend.at[t, o], prec.at[t, o], ps.at[t, o], pr.at[t, o], sibling)

        def to_chip(o):
            return remote(csend.at[t, o], crec.at[t, o], cs.at[t, o], cr.at[t, o], (r, chip(o) * 2 + k))

        def summed(o):
            to_sibling(o).wait_recv()
            return pown[o] + prec[t, o].astype(f32)

        def finish(o):
            csend[t, o] = summed(o).astype(bf16)
            to_chip(o).start()

        def step(i, _):
            o = N_CHIP - 1 - i
            psend[t, o] = forward(chip(o) * 2 + 1 - k).astype(bf16)
            to_sibling(o).start()
            pown[o] = forward(chip(o) * 2 + k)

            @pl.when(i > 0)
            def _():
                finish(o + 1)

            return 0

        lax.fori_loop(0, N_CHIP, step, 0)
        rows = summed(0)
        for o in range(N_CHIP - 1, 0, -1):
            to_chip(o).wait_recv()
            rows += crec[t, o].astype(f32)
        s[t, c] = (rows * weights[...]).astype(bf16)

        def direct(o):
            return remote(s.at[t, c], s.at[t, c], ss.at[t, o], sr.at[t, o], (r, chip(o) * 2 + k))

        def direct_in(o):
            j = chip_from(o) * 2 + k
            return remote(s.at[t, j], s.at[t, j], ss.at[t, o], sr.at[t, o], sibling)

        def across(o):
            j = chip_from(o) * 2 + k
            return remote(s.at[t, j], s.at[t, j], fs.at[t, o], fr.at[t, o], sibling)

        def across_in(o):
            j = chip_from(o) * 2 + 1 - k
            return remote(s.at[t, j], s.at[t, j], fs.at[t, o], fr.at[t, o], sibling)

        for o in range(1, N_CHIP):
            direct(o).start()
        across(0).start()

        def image(o):
            return remote(isend.at[t, o], irec.at[t, o], ims.at[t, o], imr.at[t, o], (rowdev(o), c))

        def stage(g):
            for o in (2 * g, 2 * g + 1):
                if o > 0:
                    direct_in(o).wait_recv()
                    across(o).start()

        stage(0)
        for g in range(4):
            if g < 3:
                stage(g + 1)
            for o in (2 * g, 2 * g + 1):
                across_in(o).wait_recv()
            js = [chip_from(o) * 2 + kk for o in (2 * g, 2 * g + 1) for kk in (0, 1)]

            def backward(i, _, g=g, js=js):
                o = (i + 1) % N_ROW
                p = rowdev(o)
                out = dot(s[t, js[0]], tile(x, table, js[0], p, False))
                for j in js[1:]:
                    out += dot(s[t, j], tile(x, table, j, p, False))
                if g > 0:
                    out += acc[o]
                if g < 3:
                    acc[o] = out
                else:

                    @pl.when(i < N_ROW - 1)
                    def _():
                        isend[t, o] = out.astype(bf16)
                        image(o).start()

                    @pl.when(i == N_ROW - 1)
                    def _():
                        acc[0] = out

                return 0

            lax.fori_loop(0, N_ROW, backward, 0)

        features = acc[0]
        for o in range(1, N_ROW):
            image(o).wait_recv()
            features += irec[t, o].astype(f32)
        rounded = features.astype(bf16)
        u[t, r] = rounded
        mine_d = d[r]
        mine_r = res[r]
        w = rounded.astype(f32) + RIDGE * mine_d
        sums = [total(mine_d * w), total(mine_r * w), total(w * w), rr[0:1]]
        sc1[t, 0] = jnp.concatenate(sums + [jnp.zeros((4, DIRS), f32)], axis=0)

        def scalars1(o):
            return remote(sc1.at[t, 0], sc1.at[t, o], s1s.at[t, o], s1r.at[t, o], (r, (c + o) % N_COL))

        def scalars2(o):
            return remote(sc2.at[t, 0], sc2.at[t, o], s2s.at[t, o], s2r.at[t, o], (rowdev(o), c))

        def update_out(o):
            return remote(u.at[t, r], u.at[t, r], us.at[t, o], ur.at[t, o], (rowdev(o), c))

        def update_in(o):
            p = rowdev_from(o)
            return remote(u.at[t, p], u.at[t, p], us.at[t, o], ur.at[t, o], (rowdev(o), c))

        for o in range(1, N_COL):
            scalars1(o).start()
        for o in range(1, N_ROW):
            update_out(o).start()
        both = sc1[t, 0]
        for o in range(1, N_COL):
            scalars1(o).wait_recv()
            both += sc1[t, o]
        sc2[t, 0] = both
        for o in range(1, N_ROW):
            scalars2(o).start()
        for o in range(1, N_ROW):
            scalars2(o).wait_recv()
            both += sc2[t, o]
        curvature, cross, square = both[0:1], both[1:2], both[2:3]
        now = jnp.where(t == 0, both[3:4], rr[0:1])
        alpha = now / curvature
        later = now - 2.0 * alpha * cross + alpha * alpha * square
        rr[...] = jnp.broadcast_to(later, (8, DIRS))
        coef[0] = spread(alpha)
        coef[1] = spread(later / now)

        def update(p):
            piece, alpha, beta = d[p], coef[0], coef[1]
            w = u[t, p].astype(f32) + RIDGE * piece
            sol[p] = sol[p] + alpha * piece
            rest = res[p] - alpha * w
            res[p] = rest
            ahead = rest + beta * piece
            d[p] = ahead
            v[p] = ahead.astype(bf16)

        update(r)
        for o in range(1, N_ROW):
            update_in(o).wait_recv()
            update(rowdev_from(o))
        return 0

    lax.fori_loop(0, ITERS, iteration, 0)

    def drain(t, _):
        for o in range(N_CHIP):
            remote(psend.at[t, o], prec.at[t, o], ps.at[t, o], pr.at[t, o], sibling).wait_send()
            remote(s.at[t, c], s.at[t, c], fs.at[t, o], fr.at[t, o], sibling).wait_send()
        for o in range(1, N_CHIP):
            remote(csend.at[t, o], crec.at[t, o], cs.at[t, o], cr.at[t, o], sibling).wait_send()
            remote(s.at[t, c], s.at[t, c], ss.at[t, o], sr.at[t, o], sibling).wait_send()
            remote(isend.at[t, o], irec.at[t, o], ims.at[t, o], imr.at[t, o], sibling).wait_send()
            remote(u.at[t, r], u.at[t, r], us.at[t, o], ur.at[t, o], sibling).wait_send()
            remote(sc2.at[t, 0], sc2.at[t, o], s2s.at[t, o], s2r.at[t, o], sibling).wait_send()
        for o in range(1, N_COL):
            remote(sc1.at[t, 0], sc1.at[t, o], s1s.at[t, o], s1r.at[t, o], sibling).wait_send()
        return 0

    lax.fori_loop(0, ITERS, drain, 0)


def solve(table, weights, grads, x_blocks):
    vmem = lambda *shape, dtype=bf16: pltpu.VMEM(shape, dtype)
    sems = lambda n: pltpu.SemaphoreType.DMA((ITERS, n))
    piece = (DIRS, PIECE)
    shape = jax.ShapeDtypeStruct((N_ROW, *piece), f32)
    return pl.pallas_call(
        kernel,
        out_shape=(shape, shape),
        in_specs=[
            pl.BlockSpec(memory_space=pltpu.SMEM),
            pl.BlockSpec(memory_space=pltpu.VMEM),
            pl.BlockSpec(memory_space=pltpu.VMEM),
            pl.BlockSpec(memory_space=pl.ANY),
        ],
        out_specs=(pl.BlockSpec(memory_space=pltpu.VMEM), pl.BlockSpec(memory_space=pltpu.VMEM)),
        scratch_shapes=[
            vmem(NBLK + 1, BLK, BLK),
            vmem(NBLK + 1, BLK, BLK),
            vmem(N_ROW, *piece, dtype=f32),
            vmem(N_ROW, *piece),
            vmem(ITERS, N_CHIP, *piece),
            vmem(ITERS, N_CHIP, *piece),
            vmem(N_CHIP, *piece, dtype=f32),
            vmem(ITERS, N_CHIP, *piece),
            vmem(ITERS, N_CHIP, *piece),
            vmem(ITERS, N_COL, *piece),
            vmem(N_ROW, *piece, dtype=f32),
            vmem(ITERS, N_ROW, *piece),
            vmem(ITERS, N_ROW, *piece),
            vmem(ITERS, N_ROW, *piece),
            vmem(ITERS, N_COL, 8, DIRS, dtype=f32),
            vmem(ITERS, N_ROW, 8, DIRS, dtype=f32),
            vmem(8, DIRS, dtype=f32),
            vmem(2, *piece, dtype=f32),
            pltpu.SemaphoreType.DMA((8,)),
            *[sems(8)] * 12,
            *[sems(16)] * 2,
            *[sems(8)] * 2,
        ],
        compiler_params=pltpu.CompilerParams(
            collective_id=0, has_side_effects=True, vmem_limit_bytes=60 * 2**20
        ),
    )(table, weights, grads, x_blocks)


def on_device(x_blocks, block_ids, margins, deleted, grads):
    ids = block_ids[:, 0]
    hit = jnp.arange(RB * FB, dtype=jnp.int32)[:, None] == ids[None, :]
    table = NBLK + jnp.sum(jnp.where(hit, jnp.arange(NBLK, dtype=jnp.int32)[None, :] - NBLK, 0), axis=1)
    r, c = lax.axis_index("row"), lax.axis_index("col")
    own = lax.dynamic_slice_in_dim(margins, c * PIECE, PIECE, 0)
    own_ids = r * margins.shape[0] + c * PIECE + jnp.arange(PIECE, dtype=jnp.int32)
    removed = jnp.any(own_ids[:, None] == deleted[None, :], axis=1)
    logistic = jax.nn.sigmoid(own)
    weights = jnp.where(removed, 0.0, logistic * (1.0 - logistic))[None, :]
    turned = grads.reshape(N_ROW, PIECE, DIRS).transpose(0, 2, 1)
    sol, res = solve(table, weights, turned, x_blocks)
    back = lambda a: a.transpose(0, 2, 1).reshape(N_ROW * PIECE, DIRS)
    return back(sol), back(res)


def solution(mesh):
    in_specs = (P("row", "col", None), P("row", "col"), P("row"), P("row"), P("col", None))
    out_specs = (P("col", None), P("col", None))
    return jax.shard_map(on_device, mesh=mesh, in_specs=in_specs, out_specs=out_specs, check_vma=False)
```

time: 726 us -> 172 us (0.24); the launches traced: 715 us -> 171 us
  blocking collectives: 280 us -> 0 us
  Pallas kernels: 0 us -> 159 us
  local copies, waits for them, and re-layouts: 166 us -> 7.59 us
  matrix products: 138 us -> 0 us
  waiting for transfers between devices: 89.1 us -> 0 us
  starting transfers between devices: 18.3 us -> 0 us
  between operations: 14.7 us -> 0.66 us
    all_to_all x9 -> x0, blocking collectives: 187 us -> none  [the longest x5 118 us: sent_and_summed(): lax.all_to_all(pieces, axis, split_axis=0, concat_axis=0, tiled=True)]
    pallas_call x0 -> x1, Pallas kernels: none -> 159 us  [solve(): pl.pallas_call(kernel, out_shape=(shape, shape), in_specs=[pl.BlockSpec(m...]
    dot_general x12 -> x0, matrix products: 138 us -> none  [the longest x3 43.1 us: on_device(): jnp.einsum('bji,bjk->bik', x_blocks, picked_rows, preferred_element_type=...]
    dot_general x12 -> x0, local copies, waits for them, and re-layouts: 111 us -> none  [the longest x3 52.4 us: on_device(): jnp.einsum('bij,bjk->bik', x_blocks, picked_tiles, preferred_element_type...]
    psum x15 -> x0, blocking collectives: 93.2 us -> none  [by_axis(): shard = lax.psum(shard, axis)]
    all_to_all x3 -> x0, waiting for transfers between devices: 54.1 us -> none  [the longest x1 27.5 us: sent_and_summed(): lax.all_to_all(pieces, axis, split_axis=0, concat_axis=0, tiled=True)]
    gather x6 -> x0, local copies, waits for them, and re-layouts: 51.6 us -> none  [the longest x3 25.9 us: on_device(): picked_rows = scaled[block_row]]
    all_gather x1 -> x0, waiting for transfers between devices: 35 us -> none  [in_one_piece(): result, at, outs = (lax.all_gather(both, axis, axis=dim, tiled=True), 0, [])]
  transfers between devices with their start and end apart: 4 -> 0, of which waited for: 4 -> 0; matrix products, arithmetic and copies ran while one was open for 0% -> 0% of each run, Pallas kernels for 0% -> 0%
where the time goes in v1:
time: 172 us; the launch traced here: 171 us
  Pallas kernels  159 us (92%)
  local copies, waits for them, and re-layouts  7.59 us (4%)
  other arithmetic  3.68 us (2%)
    pallas_call x1, Pallas kernels, solve(): pl.pallas_call(kernel, out_shape=(shape, shape), in_specs=[pl.BlockSpec(m...  159 us
    transpose x2, local copies, waits for them, and re-layouts, on_device(): back = lambda a: a.transpose(0, 2, 1).reshape(N_ROW * PIECE, DIRS)  5.06 us

profile of v1, /device:TPU:0, one launch (start us, length us, event | category | flops | bytes accessed | tf_op | source)
XLA Modules:
  0.0 170.9 jit_solution(5331805484721243571)
XLA Ops:
  0.6 0.9 compare_reduce_fusion
  1.5 1.4 fusion
  2.9 0.8 select_reduce_fusion
  3.7 0.6 broadcast_add_fusion.table
  4.3 2.5 %copy.10 = f32[8,256,128]{1,2,0:T(8,128)} copy(f32[8,256,128]{2,1,0:T(8,128)} %bitcast.9) | data formatting | bytes 2097152 | tf_op jit(solution)/shard_map/reshape | solution.py:345
  6.9 158.9 %shard_map.68 = (f32[8,128,256]{2,1,0:T(8,128)}, f32[8,128,256]{2,1,0:T(8,128)}) custom-call(s32[512]{0:T(512)} %broadcast_add_fusion.table, f32[1,256]{1,0:T(1,128)} %bitcast.14, f32[8,128,256]{2,1,0:T(8,128)} %bitcast.8, bf16[256,128,128]{2,1,0:T(8,128)(2,1)} %x_hbm.1), custom_call_target="tpu_custom_call" | custom-call | tf_op jit(solution)/shard_map/pallas_call | solution.py:295
  165.8 2.5 %copy.11 = f32[8,256,128]{2,1,0:T(8,128)} copy(f32[8,256,128]{1,2,0:T(8,128)} %bitcast.13) | data formatting | bytes 2097152 | tf_op jit(solution)/shard_map/transpose | solution.py:347
  168.3 2.5 %copy.12 = f32[8,256,128]{2,1,0:T(8,128)} copy(f32[8,256,128]{1,2,0:T(8,128)} %bitcast.12) | data formatting | bytes 2097152 | tf_op jit(solution)/shard_map/transpose | solution.py:347
  (2 shorter events, 0.0 us)

commit v2 on v1

v2 whole, which is shorter than its diff:
```python
import jax
import jax.numpy as jnp
from jax import lax
from jax.experimental import pallas as pl
from jax.experimental.pallas import tpu as pltpu
from jax.sharding import PartitionSpec as P

ITERS = 3
RIDGE = 0.2
N_ROW, N_COL, N_CHIP = 8, 16, 8
BLK, DIRS, FB, RB, NBLK = 128, 128, 16, 32, 256
PIECE = 256
HALF = DIRS // 2
f32, bf16 = jnp.float32, jnp.bfloat16
MESH = pl.DeviceIdType.MESH


def tile(x, table, j, p, across):
    at = lambda a, b: x[table[(2 * j + a) * FB + 2 * p + b]]
    if across:
        top = jnp.concatenate([at(0, 0), at(1, 0)], axis=1)
        low = jnp.concatenate([at(0, 1), at(1, 1)], axis=1)
    else:
        top = jnp.concatenate([at(0, 0), at(0, 1)], axis=1)
        low = jnp.concatenate([at(1, 0), at(1, 1)], axis=1)
    return jnp.concatenate([top, low], axis=0)


def dot(a, b):
    return jnp.dot(a, b, preferred_element_type=f32)


def totals(one, two):
    fold = lambda a: a[:, :BLK] + a[:, BLK:]
    row = jnp.sum(jnp.concatenate([fold(one), fold(two)], axis=0).T, axis=0, keepdims=True)
    return jnp.broadcast_to(row, (8, DIRS))


def spread(rows):
    square = jnp.broadcast_to(rows[0:1], (DIRS, DIRS)).T
    return square[:HALF], square[HALF:]


def wide(a):
    return jnp.concatenate([a, a], axis=1)


def kernel(
    table, weights, grads, x_hbm, out_sol, out_res,
    x, xt, sol, res, d, v, psend, prec, pown, csend, crec, proj, s, acc, isend, irec, u,
    a1, a2, b1, b2, rr, alpha, beta,
    xsem, ps, pr, cs, cr, fs, fr, ss, sr, ims, imr, us, ur, a1s, a1r, b1s, b1r, a2s, a2r, b2s, b2r,
):
    r, c = lax.axis_index("row"), lax.axis_index("col")
    q, k = c // 2, c % 2
    sibling = (r, q * 2 + 1 - k)

    def chip(o):
        return ((q // 2 + o // 2) % 4) * 2 + (q % 2 + o % 2) % 2

    def chip_from(o):
        return ((q // 2 + 4 - o // 2) % 4) * 2 + (q % 2 + o % 2) % 2

    def rowdev(o):
        return ((r // 4 + o // 4) % 2) * 4 + (r % 4 + o % 4) % 4

    def rowdev_from(o):
        return ((r // 4 + o // 4) % 2) * 4 + (r % 4 + 4 - o % 4) % 4

    def remote(src, dst, send, recv, to):
        return pltpu.make_async_remote_copy(
            src_ref=src, dst_ref=dst, send_sem=send, recv_sem=recv, device_id=to, device_id_type=MESH
        )

    barrier = pltpu.get_barrier_semaphore()
    for o in range(1, N_ROW):
        pl.semaphore_signal(barrier, inc=1, device_id=(rowdev(o), c), device_id_type=MESH)
    for o in range(1, N_COL):
        pl.semaphore_signal(barrier, inc=1, device_id=(r, (c + o) % N_COL), device_id_type=MESH)

    parts = 8
    size = NBLK // parts
    loads = [
        pltpu.make_async_copy(x_hbm.at[pl.ds(i * size, size)], x.at[pl.ds(i * size, size)], xsem.at[i])
        for i in range(parts)
    ]
    for load in loads:
        load.start()
    x[NBLK] = jnp.zeros((BLK, BLK), bf16)
    xt[NBLK] = jnp.zeros((BLK, BLK), bf16)

    zero = jnp.zeros((HALF, PIECE), f32)

    def begin(p, _):
        turned = grads[pl.ds(pl.multiple_of(p * PIECE, PIECE), PIECE), :].T
        for h in range(2):
            piece = turned[h * HALF : (h + 1) * HALF]
            res[h, p] = piece
            v[h, p] = piece.astype(bf16)
            d[h, p] = zero
            sol[h, p] = zero
        return 0

    lax.fori_loop(0, N_ROW, begin, 0)
    for h in range(2):
        proj[h] = zero
        beta[h] = zero
    for i in range(parts):
        loads[i].wait()

        def turn(b, _, i=i):
            xt[i * size + b] = x[i * size + b].T
            return 0

        lax.fori_loop(0, size, turn, 0, unroll=4)

    pl.semaphore_wait(barrier, N_ROW - 1 + N_COL - 1)

    def to_sibling(t, h, o):
        return remote(psend.at[t, h, o], prec.at[t, h, o], ps.at[t, h, o], pr.at[t, h, o], sibling)

    def to_chip(t, h, o):
        return remote(
            csend.at[t, h, o], crec.at[t, h, o], cs.at[t, h, o], cr.at[t, h, o], (r, chip(o) * 2 + k)
        )

    def direct(t, h, o, j):
        return remote(s.at[t, h, j], s.at[t, h, j], ss.at[t, h, o], sr.at[t, h, o], (r, chip(o) * 2 + k))

    def across(t, h, o, j):
        return remote(s.at[t, h, j], s.at[t, h, j], fs.at[t, h, o], fr.at[t, h, o], sibling)

    def image(t, h, o):
        return remote(isend.at[t, h, o], irec.at[t, h, o], ims.at[t, h, o], imr.at[t, h, o], (rowdev(o), c))

    def update(t, h, o, p):
        return remote(u.at[t, h, p], u.at[t, h, p], us.at[t, h, o], ur.at[t, h, o], (rowdev(o), c))

    def along_col(buf, send, recv, t, h, o):
        return remote(
            buf.at[t, h, 0], buf.at[t, h, o], send.at[t, h, o], recv.at[t, h, o], (r, (c + o) % N_COL)
        )

    def along_row(buf, send, recv, t, h, o):
        return remote(buf.at[t, h, 0], buf.at[t, h, o], send.at[t, h, o], recv.at[t, h, o], (rowdev(o), c))

    def share_col(buf, send, recv, t, h, rows):
        buf[t, h, 0] = rows
        for o in range(1, N_COL):
            along_col(buf, send, recv, t, h, o).start()

    def share_row(t, h, buf1, send1, recv1, buf2, send2, recv2):
        rows = buf1[t, h, 0]
        for o in range(1, N_COL):
            along_col(buf1, send1, recv1, t, h, o).wait_recv()
            rows += buf1[t, h, o]
        buf2[t, h, 0] = rows
        for o in range(1, N_ROW):
            along_row(buf2, send2, recv2, t, h, o).start()

    def collect(t, h, buf2, send2, recv2):
        rows = buf2[t, h, 0]
        for o in range(1, N_ROW):
            along_row(buf2, send2, recv2, t, h, o).wait_recv()
            rows += buf2[t, h, o]
        return spread(rows)

    def iteration(t, _):
        def forward(h, _):
            def product(j):
                out = dot(v[h, 0], tile(xt, table, j, 0, True))
                for p in range(1, N_ROW):
                    out += dot(v[h, p], tile(xt, table, j, p, True))
                return out

            def step(i, _):
                o = N_CHIP - 1 - i
                psend[t, h, o] = product(chip(o) * 2 + 1 - k).astype(bf16)
                to_sibling(t, h, o).start()
                pown[h, o] = product(chip(o) * 2 + k)

                @pl.when(i > 0)
                def _():
                    to_sibling(t, h, o + 1).wait_recv()
                    both = pown[h, o + 1] + prec[t, h, o + 1].astype(f32)
                    csend[t, h, o + 1] = both.astype(bf16)
                    to_chip(t, h, o + 1).start()

                return 0

            lax.fori_loop(0, N_CHIP, step, 0)
            return 0

        def rows_done(h, _):
            to_sibling(t, h, 0).wait_recv()
            rows = pown[h, 0] + prec[t, h, 0].astype(f32)

            @pl.when(t > 0)
            def _():
                new, _ = collect(t - 1, h, b2, b2s, b2r)
                beta[h] = wide(new / rr[h])
                rr[h] = new

            for o in range(N_CHIP - 1, 0, -1):
                to_chip(t, h, o).wait_recv()
                rows += crec[t, h, o].astype(f32)
            rows += beta[h] * proj[h]
            proj[h] = rows
            scaled = rows * weights[...]
            s[t, h, c] = scaled.astype(bf16)
            for o in range(1, N_CHIP):
                direct(t, h, o, c).start()
            across(t, h, 0, c).start()
            own = res[h, r]
            ahead = own + beta[h] * d[h, r]
            share_col(a1, a1s, a1r, t, h, totals(scaled * rows + RIDGE * ahead * ahead, own * own))
            return 0

        def backward(h, _):
            def stage(g):
                for o in (2 * g, 2 * g + 1):
                    if o > 0:
                        j = chip_from(o) * 2 + k
                        direct(t, h, o, j).wait_recv()
                        across(t, h, o, j).start()

            stage(0)
            for g in range(4):
                if g < 3:
                    stage(g + 1)
                for o in (2 * g, 2 * g + 1):
                    across(t, h, o, chip_from(o) * 2 + 1 - k).wait_recv()
                js = [chip_from(o) * 2 + kk for o in (2 * g, 2 * g + 1) for kk in (0, 1)]

                def block(i, _, g=g, js=js):
                    o = (i + 1) % N_ROW
                    p = rowdev(o)
                    out = dot(s[t, h, js[0]], tile(x, table, js[0], p, False))
                    for j in js[1:]:
                        out += dot(s[t, h, j], tile(x, table, j, p, False))
                    if g > 0:
                        out += acc[h, o]
                    if g < 3:
                        acc[h, o] = out
                    else:

                        @pl.when(i < N_ROW - 1)
                        def _():
                            isend[t, h, o] = out.astype(bf16)
                            image(t, h, o).start()

                        @pl.when(i == N_ROW - 1)
                        def _():
                            acc[h, 0] = out

                    return 0

                lax.fori_loop(0, N_ROW, block, 0)
                if g == 2:
                    share_row(t, h, a1, a1s, a1r, a2, a2s, a2r)
            return 0

        def features_done(h, _):
            curvature, first = collect(t, h, a2, a2s, a2r)

            @pl.when(t == 0)
            def _():
                rr[h] = first

            alpha[h] = wide(rr[h] / curvature)
            features = acc[h, 0]
            for o in range(1, N_ROW):
                image(t, h, o).wait_recv()
                features += irec[t, h, o].astype(f32)
            rounded = features.astype(bf16)
            u[t, h, r] = rounded
            for o in range(1, N_ROW):
                update(t, h, o, r).start()

            @pl.when(t < ITERS - 1)
            def _():
                own = res[h, r]
                ahead = own + beta[h] * d[h, r]
                own = own - alpha[h] * (u[t, h, r].astype(f32) + RIDGE * ahead)
                share_col(b1, b1s, b1r, t, h, totals(own * own, zero))

            def advance(p, _):
                ahead = res[h, p] + beta[h] * d[h, p]
                d[h, p] = ahead
                sol[h, p] = sol[h, p] + alpha[h] * ahead
                return 0

            lax.fori_loop(0, N_ROW, advance, 0)
            return 0

        def renew(h, _):
            @pl.when(t < ITERS - 1)
            def _():
                share_row(t, h, b1, b1s, b1r, b2, b2s, b2r)

            for o in range(N_ROW):
                p = rowdev_from(o)
                if o > 0:
                    update(t, h, o, p).wait_recv()
                left = res[h, p] - alpha[h] * (u[t, h, p].astype(f32) + RIDGE * d[h, p])
                res[h, p] = left
                v[h, p] = left.astype(bf16)
            return 0

        lax.fori_loop(0, 2, forward, 0)
        lax.fori_loop(0, 2, rows_done, 0)
        lax.fori_loop(0, 2, backward, 0)
        lax.fori_loop(0, 2, features_done, 0)

        @pl.when(t == ITERS - 1)
        def _():
            write(sol, out_sol)

        lax.fori_loop(0, 2, renew, 0)
        return 0

    def write(state, out):
        def turn_back(p, _):
            both = jnp.concatenate([state[0, p], state[1, p]], axis=0)
            out[pl.ds(pl.multiple_of(p * PIECE, PIECE), PIECE), :] = both.T
            return 0

        lax.fori_loop(0, N_ROW, turn_back, 0)

    lax.fori_loop(0, ITERS, iteration, 0)
    write(res, out_res)

    def drain(i, _):
        t, h = i // 2, i % 2
        for o in range(N_CHIP):
            to_sibling(t, h, o).wait_send()
            across(t, h, o, c).wait_send()
        for o in range(1, N_CHIP):
            to_chip(t, h, o).wait_send()
            direct(t, h, o, c).wait_send()
            image(t, h, o).wait_send()
            update(t, h, o, r).wait_send()
            along_row(a2, a2s, a2r, t, h, o).wait_send()
        for o in range(1, N_COL):
            along_col(a1, a1s, a1r, t, h, o).wait_send()

        @pl.when(t < ITERS - 1)
        def _():
            for o in range(1, N_ROW):
                along_row(b2, b2s, b2r, t, h, o).wait_send()
            for o in range(1, N_COL):
                along_col(b1, b1s, b1r, t, h, o).wait_send()

        return 0

    lax.fori_loop(0, 2 * ITERS, drain, 0)


def solve(table, weights, grads, x_blocks):
    vmem = lambda *shape, dtype=bf16: pltpu.VMEM(shape, dtype)
    sems = lambda n: pltpu.SemaphoreType.DMA((ITERS, 2, n))
    piece = (HALF, PIECE)
    shape = jax.ShapeDtypeStruct((N_ROW * PIECE, DIRS), f32)
    return pl.pallas_call(
        kernel,
        out_shape=(shape, shape),
        in_specs=[
            pl.BlockSpec(memory_space=pltpu.SMEM),
            pl.BlockSpec(memory_space=pltpu.VMEM),
            pl.BlockSpec(memory_space=pltpu.VMEM),
            pl.BlockSpec(memory_space=pl.ANY),
        ],
        out_specs=(pl.BlockSpec(memory_space=pltpu.VMEM), pl.BlockSpec(memory_space=pltpu.VMEM)),
        scratch_shapes=[
            vmem(NBLK + 1, BLK, BLK),
            vmem(NBLK + 1, BLK, BLK),
            vmem(2, N_ROW, *piece, dtype=f32),
            vmem(2, N_ROW, *piece, dtype=f32),
            vmem(2, N_ROW, *piece, dtype=f32),
            vmem(2, N_ROW, *piece),
            vmem(ITERS, 2, N_CHIP, *piece),
            vmem(ITERS, 2, N_CHIP, *piece),
            vmem(2, N_CHIP, *piece, dtype=f32),
            vmem(ITERS, 2, N_CHIP, *piece),
            vmem(ITERS, 2, N_CHIP, *piece),
            vmem(2, *piece, dtype=f32),
            vmem(ITERS, 2, N_COL, *piece),
            vmem(2, N_ROW, *piece, dtype=f32),
            vmem(ITERS, 2, N_ROW, *piece),
            vmem(ITERS, 2, N_ROW, *piece),
            vmem(ITERS, 2, N_ROW, *piece),
            vmem(ITERS, 2, N_COL, 8, DIRS, dtype=f32),
            vmem(ITERS, 2, N_ROW, 8, DIRS, dtype=f32),
            vmem(ITERS, 2, N_COL, 8, DIRS, dtype=f32),
            vmem(ITERS, 2, N_ROW, 8, DIRS, dtype=f32),
            vmem(2, HALF, BLK, dtype=f32),
            vmem(2, *piece, dtype=f32),
            vmem(2, *piece, dtype=f32),
            pltpu.SemaphoreType.DMA((8,)),
            *[sems(8)] * 12,
            *[sems(16)] * 4,
            *[sems(8)] * 4,
        ],
        compiler_params=pltpu.CompilerParams(
            collective_id=0, has_side_effects=True, vmem_limit_bytes=60 * 2**20
        ),
    )(table, weights, grads, x_blocks)


def on_device(x_blocks, block_ids, margins, deleted, grads):
    ids = block_ids[:, 0]
    hit = jnp.arange(RB * FB, dtype=jnp.int32)[:, None] == ids[None, :]
    table = NBLK + jnp.sum(jnp.where(hit, jnp.arange(NBLK, dtype=jnp.int32)[None, :] - NBLK, 0), axis=1)
    r, c = lax.axis_index("row"), lax.axis_index("col")
    own = lax.dynamic_slice_in_dim(margins, c * PIECE, PIECE, 0)
    own_ids = r * margins.shape[0] + c * PIECE + jnp.arange(PIECE, dtype=jnp.int32)
    removed = jnp.any(own_ids[:, None] == deleted[None, :], axis=1)
    logistic = jax.nn.sigmoid(own)
    weights = jnp.where(removed, 0.0, logistic * (1.0 - logistic))[None, :]
    return solve(table, weights, grads, x_blocks)


def solution(mesh):
    in_specs = (P("row", "col", None), P("row", "col"), P("row"), P("row"), P("col", None))
    out_specs = (P("col", None), P("col", None))
    return jax.shard_map(on_device, mesh=mesh, in_specs=in_specs, out_specs=out_specs, check_vma=False)
```

time: 172 us -> 188 us (1.093)
  Pallas kernels: 159 us -> 178 us
  local copies, waits for them, and re-layouts: 7.59 us -> 4.52 us
    pallas_call x1, Pallas kernels: 159 us -> 178 us  [solve(): pl.pallas_call(kernel, out_shape=(shape, shape), in_specs=[pl.BlockSpec(m...]
    transpose x2 -> x0, local copies, waits for them, and re-layouts: 5.06 us -> none  [on_device(): back = lambda a: a.transpose(0, 2, 1).reshape(N_ROW * PIECE, DIRS)]
    unnamed x0 -> x2, local copies, waits for them, and re-layouts: none -> 4.52 us
    reshape x1 -> x0, local copies, waits for them, and re-layouts: 2.53 us -> none  [on_device(): turned = grads.reshape(N_ROW, PIECE, DIRS).transpose(0, 2, 1)]
where the time goes in v2:
time: 188 us; the launch traced here: 187 us
  Pallas kernels  178 us (95%)
  local copies, waits for them, and re-layouts  4.52 us (2%)
  other arithmetic  3.64 us (2%)
    pallas_call x1, Pallas kernels, solve(): pl.pallas_call(kernel, out_shape=(shape, shape), in_specs=[pl.BlockSpec(m...  178 us
    unnamed x2, local copies, waits for them, and re-layouts  4.52 us

profile of v2, /device:TPU:0, one launch (start us, length us, event | category | flops | bytes accessed | tf_op | source)
XLA Modules:
  0.0 186.9 jit_solution(4853731796961755708)
XLA Ops:
  0.6 0.9 compare_reduce_fusion
  1.5 1.3 fusion
  2.9 0.8 select_reduce_fusion
  3.7 0.6 broadcast_add_fusion.table
  4.3 178.1 %shard_map.68 = (f32[2048,128]{1,0:T(8,128)}, f32[2048,128]{1,0:T(8,128)}) custom-call(s32[512]{0:T(512)} %broadcast_add_fusion.table, f32[1,256]{1,0:T(1,128)} %bitcast.2, f32[2048,128]{1,0:T(8,128)} %grads.1, bf16[256,128,128]{2,1,0:T(8,128)(2,1)} %x_hbm.1), custom_call_target="tpu_custom_call" | custom-call | tf_op jit(solution)/shard_map/pallas_call | solution.py:364
  182.4 2.3 %copy.9 = f32[2048,128]{1,0:T(8,128)} copy(f32[2048,128]{1,0:T(8,128)} %get-tuple-element.4) | data formatting | bytes 2097152
  184.6 2.3 %copy.10 = f32[2048,128]{1,0:T(8,128)} copy(f32[2048,128]{1,0:T(8,128)} %get-tuple-element.5) | data formatting | bytes 2097152
  (2 shorter events, 0.0 us)

commit v3 on v1

v3 whole, which is shorter than its diff:
```python
import jax
import jax.numpy as jnp
from jax import lax
from jax.experimental import pallas as pl
from jax.experimental.pallas import tpu as pltpu
from jax.sharding import PartitionSpec as P

ITERS = 3
RIDGE = 0.2
N_ROW, N_COL, N_CHIP = 8, 16, 8
BLK, DIRS, FB, RB, NBLK = 128, 128, 16, 32, 256
PIECE = 256
HALF = DIRS // 2
WIDTH = 2
f32, bf16 = jnp.float32, jnp.bfloat16
MESH = pl.DeviceIdType.MESH


def tile(x, table, j, p, across):
    at = lambda a, b: x[table[(2 * j + a) * FB + 2 * p + b]]
    if across:
        top = jnp.concatenate([at(0, 0), at(1, 0)], axis=1)
        low = jnp.concatenate([at(0, 1), at(1, 1)], axis=1)
    else:
        top = jnp.concatenate([at(0, 0), at(0, 1)], axis=1)
        low = jnp.concatenate([at(1, 0), at(1, 1)], axis=1)
    return jnp.concatenate([top, low], axis=0)


def dot(a, b):
    return jnp.dot(a, b, preferred_element_type=f32)


def totals(one, two):
    sums = [jnp.sum((a[:, :BLK] + a[:, BLK:]).T, axis=0, keepdims=True) for a in (one, two)]
    return jnp.concatenate(sums + [jnp.zeros((6, DIRS), f32)], axis=0)


def spread(row):
    square = jnp.broadcast_to(row, (DIRS, DIRS)).T
    return jnp.concatenate([square, square], axis=1)


def kernel(
    table, weights, grads, x_hbm, out_sol, out_res,
    x, xt, sol, res, d, v, psend, prec, pown, csend, crec, proj, s, acc, isend, irec, u,
    a1, a2, b1, b2, rr, alpha, beta,
    xsem, ps, pr, cs, cr, fs, fr, ss, sr, ims, imr, us, ur, a1s, a1r, b1s, b1r, a2s, a2r, b2s, b2r,
):
    r, c = lax.axis_index("row"), lax.axis_index("col")
    q, k = c // 2, c % 2
    sibling = (r, q * 2 + 1 - k)

    def chip(o):
        return ((q // 2 + o // 2) % 4) * 2 + (q % 2 + o % 2) % 2

    def chip_from(o):
        return ((q // 2 + 4 - o // 2) % 4) * 2 + (q % 2 + o % 2) % 2

    def rowdev(o):
        return ((r // 4 + o // 4) % 2) * 4 + (r % 4 + o % 4) % 4

    def rowdev_from(o):
        return ((r // 4 + o // 4) % 2) * 4 + (r % 4 + 4 - o % 4) % 4

    def remote(src, dst, send, recv, to):
        return pltpu.make_async_remote_copy(
            src_ref=src, dst_ref=dst, send_sem=send, recv_sem=recv, device_id=to, device_id_type=MESH
        )

    barrier = pltpu.get_barrier_semaphore()
    for o in range(1, N_ROW):
        pl.semaphore_signal(barrier, inc=1, device_id=(rowdev(o), c), device_id_type=MESH)
    for o in range(1, N_COL):
        pl.semaphore_signal(barrier, inc=1, device_id=(r, (c + o) % N_COL), device_id_type=MESH)

    parts = 8
    size = NBLK // parts
    loads = [
        pltpu.make_async_copy(x_hbm.at[pl.ds(i * size, size)], x.at[pl.ds(i * size, size)], xsem.at[i])
        for i in range(parts)
    ]
    for load in loads:
        load.start()
    x[NBLK] = jnp.zeros((BLK, BLK), bf16)
    xt[NBLK] = jnp.zeros((BLK, BLK), bf16)

    zero = jnp.zeros((DIRS, PIECE), f32)

    def begin(p, _):
        turned = grads[pl.ds(pl.multiple_of(p * PIECE, PIECE), PIECE), :].T
        res[p] = turned
        v[p] = turned.astype(bf16)
        d[p] = zero
        sol[p] = zero
        return 0

    lax.fori_loop(0, N_ROW, begin, 0)
    proj[...] = zero
    beta[...] = zero
    for i in range(parts):
        loads[i].wait()

        def turn(b, _, i=i):
            xt[i * size + b] = x[i * size + b].T
            return 0

        lax.fori_loop(0, size, turn, 0, unroll=4)

    pl.semaphore_wait(barrier, N_ROW - 1 + N_COL - 1)

    def to_sibling(t, o):
        return remote(psend.at[t, o], prec.at[t, o], ps.at[t, o], pr.at[t, o], sibling)

    def to_chip(t, o):
        return remote(csend.at[t, o], crec.at[t, o], cs.at[t, o], cr.at[t, o], (r, chip(o) * 2 + k))

    def direct(t, o, j):
        return remote(s.at[t, j], s.at[t, j], ss.at[t, o], sr.at[t, o], (r, chip(o) * 2 + k))

    def across(t, o, j):
        return remote(s.at[t, j], s.at[t, j], fs.at[t, o], fr.at[t, o], sibling)

    def image(t, h, o):
        return remote(isend.at[t, h, o], irec.at[t, h, o], ims.at[t, h, o], imr.at[t, h, o], (rowdev(o), c))

    def update(t, h, o, p):
        return remote(u.at[t, h, p], u.at[t, h, p], us.at[t, h, o], ur.at[t, h, o], (rowdev(o), c))

    def along_col(buf, send, recv, t, o):
        return remote(buf.at[t, 0], buf.at[t, o], send.at[t, o], recv.at[t, o], (r, (c + o) % N_COL))

    def along_row(buf, send, recv, t, o):
        return remote(buf.at[t, 0], buf.at[t, o], send.at[t, o], recv.at[t, o], (rowdev(o), c))

    def share_col(buf, send, recv, t, rows):
        buf[t, 0] = rows
        for o in range(1, N_COL):
            along_col(buf, send, recv, t, o).start()

    def share_row(t, buf1, send1, recv1, buf2, send2, recv2):
        rows = buf1[t, 0]
        for o in range(1, N_COL):
            along_col(buf1, send1, recv1, t, o).wait_recv()
            rows += buf1[t, o]
        buf2[t, 0] = rows
        for o in range(1, N_ROW):
            along_row(buf2, send2, recv2, t, o).start()

    def collect(t, buf2, send2, recv2):
        rows = buf2[t, 0]
        for o in range(1, N_ROW):
            along_row(buf2, send2, recv2, t, o).wait_recv()
            rows += buf2[t, o]
        return rows

    def iteration(t, _):
        def product(j):
            out = dot(v[0], tile(xt, table, j, 0, True))
            for p in range(1, N_ROW):
                out += dot(v[p], tile(xt, table, j, p, True))
            return out

        def chip_sum(o):
            to_sibling(t, o).wait_recv()
            return pown[o] + prec[t, o].astype(f32)

        def send_sum(o):
            csend[t, o] = chip_sum(o).astype(bf16)
            to_chip(t, o).start()

        def forward(i, _):
            chips = [N_CHIP - 1 - WIDTH * i - w for w in range(WIDTH)]
            theirs = [product(chip(o) * 2 + 1 - k) for o in chips]
            mine = [product(chip(o) * 2 + k) for o in chips]
            for o, piece in zip(chips, theirs):
                psend[t, o] = piece.astype(bf16)
                to_sibling(t, o).start()
            for o, piece in zip(chips, mine):
                pown[o] = piece

            @pl.when(i > 0)
            def _():
                for o in chips:
                    send_sum(o + WIDTH)

            return 0

        lax.fori_loop(0, N_CHIP // WIDTH, forward, 0)
        for o in range(WIDTH - 1, 0, -1):
            send_sum(o)
        rows = chip_sum(0)

        @pl.when(t > 0)
        def _():
            sums = collect(t - 1, b2, b2s, b2r)
            beta[...] = spread(sums[0:1] / rr[0:1])
            rr[...] = jnp.broadcast_to(sums[0:1], (8, DIRS))

        rows += beta[...] * proj[...]
        for o in range(N_CHIP - 1, 0, -1):
            to_chip(t, o).wait_recv()
            rows += crec[t, o].astype(f32)
        scaled = rows * weights[...]
        s[t, c] = scaled.astype(bf16)
        across(t, 0, c).start()
        for o in range(1, N_CHIP):
            direct(t, o, c).start()
        proj[...] = rows
        own = res[r]
        ahead = own + beta[...] * d[r]
        share_col(a1, a1s, a1r, t, totals(scaled * rows + RIDGE * ahead * ahead, own * own))

        def stage(g):
            for o in (2 * g, 2 * g + 1):
                if o > 0:
                    j = chip_from(o) * 2 + k
                    direct(t, o, j).wait_recv()
                    across(t, o, j).start()

        stage(0)
        for g in range(4):
            if g < 3:
                stage(g + 1)
            for o in (2 * g, 2 * g + 1):
                across(t, o, chip_from(o) * 2 + 1 - k).wait_recv()
            js = [chip_from(o) * 2 + kk for o in (2 * g, 2 * g + 1) for kk in (0, 1)]
            outs = []
            for o in range(N_ROW):
                p = rowdev(o)
                out = dot(s[t, js[0]], tile(x, table, js[0], p, False))
                for j in js[1:]:
                    out += dot(s[t, j], tile(x, table, j, p, False))
                outs.append(out)
            for o in range(N_ROW):
                if g > 0:
                    outs[o] += acc[o]
                if g < 3 or o == 0:
                    acc[o] = outs[o]
                else:
                    isend[t, 0, o] = outs[o][:HALF].astype(bf16)
                    isend[t, 1, o] = outs[o][HALF:].astype(bf16)
                    image(t, 0, o).start()
        for o in range(1, N_ROW):
            image(t, 1, o).start()
        share_row(t, a1, a1s, a1r, a2, a2s, a2r)

        for h in range(2):
            half = pl.ds(h * HALF, HALF)
            features = acc[0, half]
            for o in range(1, N_ROW):
                image(t, h, o).wait_recv()
                features += irec[t, h, o].astype(f32)
            u[t, h, r] = features.astype(bf16)
            for o in range(1, N_ROW):
                update(t, h, o, r).start()

        sums = collect(t, a2, a2s, a2r)

        @pl.when(t == 0)
        def _():
            rr[...] = jnp.broadcast_to(sums[1:2], (8, DIRS))

        alpha[...] = spread(rr[0:1] / sums[0:1])

        @pl.when(t < ITERS - 1)
        def _():
            gone = jnp.concatenate([u[t, 0, r], u[t, 1, r]], axis=0).astype(f32)
            own = res[r]
            own = own - alpha[...] * (gone + RIDGE * (own + beta[...] * d[r]))
            share_col(b1, b1s, b1r, t, totals(own * own, zero))

        def advance(p, _):
            ahead = res[p] + beta[...] * d[p]
            d[p] = ahead
            sol[p] = sol[p] + alpha[...] * ahead
            return 0

        lax.fori_loop(0, N_ROW, advance, 0)

        @pl.when(t == ITERS - 1)
        def _():
            write(sol, out_sol)

        for h in range(2):
            half = pl.ds(h * HALF, HALF)

            def renew(o, _, h=h, half=half):
                p = rowdev_from(o)

                @pl.when(o > 0)
                def _():
                    update(t, h, o, p).wait_recv()

                left = res[p, half] - alpha[half] * (u[t, h, p].astype(f32) + RIDGE * d[p, half])
                res[p, half] = left
                v[p, half] = left.astype(bf16)
                return 0

            lax.fori_loop(0, N_ROW, renew, 0)

        @pl.when(t < ITERS - 1)
        def _():
            share_row(t, b1, b1s, b1r, b2, b2s, b2r)

        return 0

    def write(state, out):
        def turn_back(p, _):
            out[pl.ds(pl.multiple_of(p * PIECE, PIECE), PIECE), :] = state[p].T
            return 0

        lax.fori_loop(0, N_ROW, turn_back, 0)

    lax.fori_loop(0, ITERS, iteration, 0)
    write(res, out_res)

    def drain(t, _):
        for o in range(N_CHIP):
            to_sibling(t, o).wait_send()
            across(t, o, c).wait_send()
        for o in range(1, N_CHIP):
            to_chip(t, o).wait_send()
            direct(t, o, c).wait_send()
            along_row(a2, a2s, a2r, t, o).wait_send()
            for h in range(2):
                image(t, h, o).wait_send()
                update(t, h, o, r).wait_send()
        for o in range(1, N_COL):
            along_col(a1, a1s, a1r, t, o).wait_send()

        @pl.when(t < ITERS - 1)
        def _():
            for o in range(1, N_ROW):
                along_row(b2, b2s, b2r, t, o).wait_send()
            for o in range(1, N_COL):
                along_col(b1, b1s, b1r, t, o).wait_send()

        return 0

    lax.fori_loop(0, ITERS, drain, 0)


def solve(table, weights, grads, x_blocks):
    vmem = lambda *shape, dtype=bf16: pltpu.VMEM(shape, dtype)
    sems = lambda *n: pltpu.SemaphoreType.DMA((ITERS, *n))
    piece, half = (DIRS, PIECE), (HALF, PIECE)
    shape = jax.ShapeDtypeStruct((N_ROW * PIECE, DIRS), f32)
    return pl.pallas_call(
        kernel,
        out_shape=(shape, shape),
        in_specs=[
            pl.BlockSpec(memory_space=pltpu.SMEM),
            pl.BlockSpec(memory_space=pltpu.VMEM),
            pl.BlockSpec(memory_space=pltpu.VMEM),
            pl.BlockSpec(memory_space=pl.ANY),
        ],
        out_specs=(pl.BlockSpec(memory_space=pltpu.VMEM), pl.BlockSpec(memory_space=pltpu.VMEM)),
        scratch_shapes=[
            vmem(NBLK + 1, BLK, BLK),
            vmem(NBLK + 1, BLK, BLK),
            vmem(N_ROW, *piece, dtype=f32),
            vmem(N_ROW, *piece, dtype=f32),
            vmem(N_ROW, *piece, dtype=f32),
            vmem(N_ROW, *piece),
            vmem(ITERS, N_CHIP, *piece),
            vmem(ITERS, N_CHIP, *piece),
            vmem(N_CHIP, *piece, dtype=f32),
            vmem(ITERS, N_CHIP, *piece),
            vmem(ITERS, N_CHIP, *piece),
            vmem(*piece, dtype=f32),
            vmem(ITERS, N_COL, *piece),
            vmem(N_ROW, *piece, dtype=f32),
            vmem(ITERS, 2, N_ROW, *half),
            vmem(ITERS, 2, N_ROW, *half),
            vmem(ITERS, 2, N_ROW, *half),
            vmem(ITERS, N_COL, 8, DIRS, dtype=f32),
            vmem(ITERS, N_ROW, 8, DIRS, dtype=f32),
            vmem(ITERS, N_COL, 8, DIRS, dtype=f32),
            vmem(ITERS, N_ROW, 8, DIRS, dtype=f32),
            vmem(8, DIRS, dtype=f32),
            vmem(*piece, dtype=f32),
            vmem(*piece, dtype=f32),
            pltpu.SemaphoreType.DMA((8,)),
            *[sems(8)] * 8,
            *[sems(2, 8)] * 4,
            *[sems(16)] * 4,
            *[sems(8)] * 4,
        ],
        compiler_params=pltpu.CompilerParams(
            collective_id=0, has_side_effects=True, vmem_limit_bytes=60 * 2**20
        ),
    )(table, weights, grads, x_blocks)


def on_device(x_blocks, block_ids, margins, deleted, grads):
    ids = block_ids[:, 0]
    hit = jnp.arange(RB * FB, dtype=jnp.int32)[:, None] == ids[None, :]
    table = NBLK + jnp.sum(jnp.where(hit, jnp.arange(NBLK, dtype=jnp.int32)[None, :] - NBLK, 0), axis=1)
    r, c = lax.axis_index("row"), lax.axis_index("col")
    own = lax.dynamic_slice_in_dim(margins, c * PIECE, PIECE, 0)
    own_ids = r * margins.shape[0] + c * PIECE + jnp.arange(PIECE, dtype=jnp.int32)
    removed = jnp.any(own_ids[:, None] == deleted[None, :], axis=1)
    logistic = jax.nn.sigmoid(own)
    weights = jnp.where(removed, 0.0, logistic * (1.0 - logistic))[None, :]
    return solve(table, weights, grads, x_blocks)


def solution(mesh):
    in_specs = (P("row", "col", None), P("row", "col"), P("row"), P("row"), P("col", None))
    out_specs = (P("col", None), P("col", None))
    return jax.shard_map(on_device, mesh=mesh, in_specs=in_specs, out_specs=out_specs, check_vma=False)
```

time: 172 us -> 149 us (0.87)
  Pallas kernels: 159 us -> 140 us
  local copies, waits for them, and re-layouts: 7.59 us -> 4.52 us
    pallas_call x1, Pallas kernels: 159 us -> 140 us  [solve(): pl.pallas_call(kernel, out_shape=(shape, shape), in_specs=[pl.BlockSpec(m...]
    transpose x2 -> x0, local copies, waits for them, and re-layouts: 5.06 us -> none  [on_device(): back = lambda a: a.transpose(0, 2, 1).reshape(N_ROW * PIECE, DIRS)]
    unnamed x0 -> x2, local copies, waits for them, and re-layouts: none -> 4.52 us
    reshape x1 -> x0, local copies, waits for them, and re-layouts: 2.53 us -> none  [on_device(): turned = grads.reshape(N_ROW, PIECE, DIRS).transpose(0, 2, 1)]
where the time goes in v3:
time: 149 us
  Pallas kernels  140 us (94%)
  local copies, waits for them, and re-layouts  4.52 us (3%)
  other arithmetic  3.64 us (2%)
    pallas_call x1, Pallas kernels, solve(): pl.pallas_call(kernel, out_shape=(shape, shape), in_specs=[pl.BlockSpec(m...  140 us
    unnamed x2, local copies, waits for them, and re-layouts  4.52 us

profile of v3, /device:TPU:0, one launch (start us, length us, event | category | flops | bytes accessed | tf_op | source)
XLA Modules:
  0.0 149.0 jit_solution(16836039792257226033)
XLA Ops:
  0.6 0.9 compare_reduce_fusion
  1.5 1.3 fusion
  2.9 0.8 select_reduce_fusion
  3.7 0.6 broadcast_add_fusion.table
  4.3 140.2 %shard_map.68 = (f32[2048,128]{1,0:T(8,128)}, f32[2048,128]{1,0:T(8,128)}) custom-call(s32[512]{0:T(512)} %broadcast_add_fusion.table, f32[1,256]{1,0:T(1,128)} %bitcast.2, f32[2048,128]{1,0:T(8,128)} %grads.1, bf16[256,128,128]{2,1,0:T(8,128)(2,1)} %x_hbm.1), custom_call_target="tpu_custom_call" | custom-call | tf_op jit(solution)/shard_map/pallas_call | solution.py:349
  144.5 2.3 %copy.9 = f32[2048,128]{1,0:T(8,128)} copy(f32[2048,128]{1,0:T(8,128)} %get-tuple-element.4) | data formatting | bytes 2097152
  146.7 2.3 %copy.10 = f32[2048,128]{1,0:T(8,128)} copy(f32[2048,128]{1,0:T(8,128)} %get-tuple-element.5) | data formatting | bytes 2097152
  (2 shorter events, 0.0 us)

commit v4 on v2

v4 whole, which is shorter than its diff:
```python
import jax
import jax.numpy as jnp
from jax import lax
from jax.experimental import pallas as pl
from jax.experimental.pallas import tpu as pltpu
from jax.sharding import PartitionSpec as P

ITERS = 3
RIDGE = 0.2
N_ROW, N_COL, N_CHIP = 8, 16, 8
BLK, DIRS, FB, RB, NBLK = 128, 128, 16, 32, 256
PIECE = 256
HALF = DIRS // 2
WIDTH = 2
CHIP_ORDER = (5, 1, 3, 7, 4, 2, 6)
ROW_ORDER = (6, 2, 5, 7, 4, 1, 3)
f32, bf16 = jnp.float32, jnp.bfloat16
MESH = pl.DeviceIdType.MESH


def tile(x, table, j, p, across):
    at = lambda a, b: x[table[(2 * j + a) * FB + 2 * p + b]]
    if across:
        top = jnp.concatenate([at(0, 0), at(1, 0)], axis=1)
        low = jnp.concatenate([at(0, 1), at(1, 1)], axis=1)
    else:
        top = jnp.concatenate([at(0, 0), at(0, 1)], axis=1)
        low = jnp.concatenate([at(1, 0), at(1, 1)], axis=1)
    return jnp.concatenate([top, low], axis=0)


def dot(a, b):
    return jnp.dot(a, b, preferred_element_type=f32)


def fold(a):
    return a[:, :BLK] + a[:, BLK:]


def total(parts):
    return jnp.sum(jnp.concatenate([parts[0], parts[1]], axis=0).T, axis=0, keepdims=True)


def packed(rows):
    return jnp.concatenate([*rows, jnp.zeros((8 - len(rows), DIRS), f32)], axis=0)


def spread(row):
    square = jnp.broadcast_to(row, (DIRS, DIRS)).T
    both = jnp.concatenate([square, square], axis=1)
    return both[:HALF], both[HALF:]


def kernel(
    table, weights, grads, x_hbm, out_sol, out_res,
    x, xt, sol, res, d, v, psend, prec, pown, csend, crec, proj, s, acc, isend, irec, u,
    a1, a2, b1, b2, part, rr, alpha, beta,
    xsem, ps, pr, cs, cr, fs, fr, ss, sr, ims, imr, us, ur, a1s, a1r, b1s, b1r, a2s, a2r, b2s, b2r,
):
    r, c = lax.axis_index("row"), lax.axis_index("col")
    q, k = c // 2, c % 2
    sibling = (r, q * 2 + 1 - k)

    def chip(o):
        return ((q // 2 + o // 2) % 4) * 2 + (q % 2 + o % 2) % 2

    def chip_from(o):
        return ((q // 2 + 4 - o // 2) % 4) * 2 + (q % 2 + o % 2) % 2

    def rowdev(o):
        return ((r // 4 + o // 4) % 2) * 4 + (r % 4 + o % 4) % 4

    def rowdev_from(o):
        return ((r // 4 + o // 4) % 2) * 4 + (r % 4 + 4 - o % 4) % 4

    def remote(src, dst, send, recv, to):
        return pltpu.make_async_remote_copy(
            src_ref=src, dst_ref=dst, send_sem=send, recv_sem=recv, device_id=to, device_id_type=MESH
        )

    barrier = pltpu.get_barrier_semaphore()
    for o in range(1, N_ROW):
        pl.semaphore_signal(barrier, inc=1, device_id=(rowdev(o), c), device_id_type=MESH)
    for o in range(1, N_COL):
        pl.semaphore_signal(barrier, inc=1, device_id=(r, (c + o) % N_COL), device_id_type=MESH)

    parts = 8
    size = NBLK // parts
    loads = [
        pltpu.make_async_copy(x_hbm.at[pl.ds(i * size, size)], x.at[pl.ds(i * size, size)], xsem.at[i])
        for i in range(parts)
    ]
    for load in loads:
        load.start()
    x[NBLK] = jnp.zeros((BLK, BLK), bf16)
    xt[NBLK] = jnp.zeros((BLK, BLK), bf16)

    zero = jnp.zeros((HALF, PIECE), f32)

    def begin(p, _):
        turned = grads[pl.ds(pl.multiple_of(p * PIECE, PIECE), PIECE), :].T
        for h in range(2):
            piece = turned[h * HALF : (h + 1) * HALF]
            res[h, p] = piece
            v[h, p] = piece.astype(bf16)
            d[h, p] = zero
            sol[h, p] = zero
        return 0

    lax.fori_loop(0, N_ROW, begin, 0)
    for h in range(2):
        proj[h] = zero
        beta[h] = zero
    for i in range(parts):
        loads[i].wait()

        def turn(b, _, i=i):
            xt[i * size + b] = x[i * size + b].T
            return 0

        lax.fori_loop(0, size, turn, 0, unroll=4)

    pl.semaphore_wait(barrier, N_ROW - 1 + N_COL - 1)

    def to_sibling(t, h, o):
        return remote(psend.at[t, h, o], prec.at[t, h, o], ps.at[t, h, o], pr.at[t, h, o], sibling)

    def to_chip(t, h, o):
        return remote(
            csend.at[t, h, o], crec.at[t, h, o], cs.at[t, h, o], cr.at[t, h, o], (r, chip(o) * 2 + k)
        )

    def direct(t, h, o, j):
        return remote(s.at[t, h, j], s.at[t, h, j], ss.at[t, h, o], sr.at[t, h, o], (r, chip(o) * 2 + k))

    def across(t, h, o, j):
        return remote(s.at[t, h, j], s.at[t, h, j], fs.at[t, h, o], fr.at[t, h, o], sibling)

    def image(t, h, o):
        return remote(isend.at[t, h, o], irec.at[t, h, o], ims.at[t, h, o], imr.at[t, h, o], (rowdev(o), c))

    def update(t, h, o, p):
        return remote(u.at[t, h, p], u.at[t, h, p], us.at[t, h, o], ur.at[t, h, o], (rowdev(o), c))

    def along_col(buf, send, recv, t, o):
        return remote(buf.at[t, 0], buf.at[t, o], send.at[t, o], recv.at[t, o], (r, (c + o) % N_COL))

    def along_row(buf, send, recv, t, o):
        return remote(buf.at[t, 0], buf.at[t, o], send.at[t, o], recv.at[t, o], (rowdev(o), c))

    def share_col(buf, send, recv, t, rows):
        buf[t, 0] = rows
        for o in range(1, N_COL):
            along_col(buf, send, recv, t, o).start()

    def share_row(t, buf1, send1, recv1, buf2, send2, recv2):
        rows = buf1[t, 0]
        for o in range(1, N_COL):
            along_col(buf1, send1, recv1, t, o).wait_recv()
            rows += buf1[t, o]
        buf2[t, 0] = rows
        for o in range(1, N_ROW):
            along_row(buf2, send2, recv2, t, o).start()

    def collect(t, buf2, send2, recv2):
        rows = buf2[t, 0]
        for o in range(1, N_ROW):
            along_row(buf2, send2, recv2, t, o).wait_recv()
            rows += buf2[t, o]
        return rows

    def renew(t, h):
        for o in (0, *ROW_ORDER):
            p = rowdev_from(o)
            if o > 0:
                update(t, h, o, p).wait_recv()
            left = res[h, p] - alpha[h] * (u[t, h, p].astype(f32) + RIDGE * d[h, p])
            res[h, p] = left
            v[h, p] = left.astype(bf16)

    def iteration(t, _):
        def forward(h, _):
            @pl.when((t > 0) & (h > 0))
            def _():
                share_row(t - 1, b1, b1s, b1r, b2, b2s, b2r)

            @pl.when(t > 0)
            def _():
                renew(t - 1, h)

            def product(j):
                out = dot(v[h, 0], tile(xt, table, j, 0, True))
                for p in range(1, N_ROW):
                    out += dot(v[h, p], tile(xt, table, j, p, True))
                return out

            def send_sum(o):
                to_sibling(t, h, o).wait_recv()
                csend[t, h, o] = (pown[h, o] + prec[t, h, o].astype(f32)).astype(bf16)
                to_chip(t, h, o).start()

            order = (*CHIP_ORDER, 0)
            for i in range(0, N_CHIP, WIDTH):
                chips = order[i : i + WIDTH]
                theirs = [product(chip(o) * 2 + 1 - k) for o in chips]
                mine = [product(chip(o) * 2 + k) for o in chips]
                for o, piece in zip(chips, theirs):
                    psend[t, h, o] = piece.astype(bf16)
                    to_sibling(t, h, o).start()
                for o, piece in zip(chips, mine):
                    pown[h, o] = piece
                if i > 0:
                    for o in order[i - WIDTH : i]:
                        send_sum(o)
            for o in order[-WIDTH:-1]:
                send_sum(o)
            return 0

        lax.fori_loop(0, 2, forward, 0)

        @pl.when(t > 0)
        def _():
            new = collect(t - 1, b2, b2s, b2r)[0:1]
            beta[0], beta[1] = spread(new / rr[0:1])
            rr[...] = jnp.broadcast_to(new, (8, DIRS))

        def rows_done(h, _):
            to_sibling(t, h, 0).wait_recv()
            rows = pown[h, 0] + prec[t, h, 0].astype(f32) + beta[h] * proj[h]
            for o in CHIP_ORDER:
                to_chip(t, h, o).wait_recv()
                rows += crec[t, h, o].astype(f32)
            scaled = rows * weights[...]
            s[t, h, c] = scaled.astype(bf16)
            for o in CHIP_ORDER:
                direct(t, h, o, c).start()
            across(t, h, 0, c).start()
            proj[h] = rows
            own = res[h, r]
            ahead = own + beta[h] * d[h, r]
            part[0, h] = fold(scaled * rows + RIDGE * ahead * ahead)
            part[1, h] = fold(own * own)
            return 0

        lax.fori_loop(0, 2, rows_done, 0)
        share_col(a1, a1s, a1r, t, packed([total(part[0]), total(part[1])]))

        def backward(h, _):
            order = (0, *CHIP_ORDER)

            def stage(g):
                for o in order[2 * g : 2 * g + 2]:
                    if o > 0:
                        j = chip_from(o) * 2 + k
                        direct(t, h, o, j).wait_recv()
                        across(t, h, o, j).start()

            stage(0)
            for g in range(4):
                if g < 3:
                    stage(g + 1)
                for o in order[2 * g : 2 * g + 2]:
                    across(t, h, o, chip_from(o) * 2 + 1 - k).wait_recv()
                js = [chip_from(o) * 2 + kk for o in order[2 * g : 2 * g + 2] for kk in (0, 1)]
                outs = []
                rows = (*ROW_ORDER, 0)
                for o in rows:
                    p = rowdev(o)
                    out = dot(s[t, h, js[0]], tile(x, table, js[0], p, False))
                    for j in js[1:]:
                        out += dot(s[t, h, j], tile(x, table, j, p, False))
                    outs.append(out)
                for o, out in zip(rows, outs):
                    if g > 0:
                        out += acc[h, o]
                    if g < 3 or o == 0:
                        acc[h, o] = out
                    else:
                        isend[t, h, o] = out.astype(bf16)
                        image(t, h, o).start()
            return 0

        lax.fori_loop(0, 2, backward, 0)
        share_row(t, a1, a1s, a1r, a2, a2s, a2r)

        def features_done(h, _):
            features = acc[h, 0]
            for o in ROW_ORDER:
                image(t, h, o).wait_recv()
                features += irec[t, h, o].astype(f32)
            u[t, h, r] = features.astype(bf16)
            for o in ROW_ORDER:
                update(t, h, o, r).start()
            return 0

        lax.fori_loop(0, 2, features_done, 0)
        sums = collect(t, a2, a2s, a2r)

        @pl.when(t == 0)
        def _():
            rr[...] = jnp.broadcast_to(sums[1:2], (8, DIRS))

        alpha[0], alpha[1] = spread(rr[0:1] / sums[0:1])

        @pl.when(t < ITERS - 1)
        def _():
            for h in range(2):
                own = res[h, r]
                ahead = own + beta[h] * d[h, r]
                own = own - alpha[h] * (u[t, h, r].astype(f32) + RIDGE * ahead)
                part[0, h] = fold(own * own)
            share_col(b1, b1s, b1r, t, packed([total(part[0])]))

        def advance(i, _):
            h, p = i // N_ROW, i % N_ROW
            ahead = res[h, p] + beta[h] * d[h, p]
            d[h, p] = ahead
            sol[h, p] = sol[h, p] + alpha[h] * ahead
            return 0

        lax.fori_loop(0, 2 * N_ROW, advance, 0, unroll=2)
        return 0

    def write(state, out):
        def turn_back(p, _):
            both = jnp.concatenate([state[0, p], state[1, p]], axis=0)
            out[pl.ds(pl.multiple_of(p * PIECE, PIECE), PIECE), :] = both.T
            return 0

        lax.fori_loop(0, N_ROW, turn_back, 0)

    lax.fori_loop(0, ITERS, iteration, 0)
    write(sol, out_sol)
    for h in range(2):
        renew(ITERS - 1, h)
    write(res, out_res)

    def drain(t, _):
        for h in range(2):
            for o in range(N_CHIP):
                to_sibling(t, h, o).wait_send()
                across(t, h, o, c).wait_send()
            for o in range(1, N_CHIP):
                to_chip(t, h, o).wait_send()
                direct(t, h, o, c).wait_send()
                image(t, h, o).wait_send()
                update(t, h, o, r).wait_send()
        for o in range(1, N_ROW):
            along_row(a2, a2s, a2r, t, o).wait_send()
        for o in range(1, N_COL):
            along_col(a1, a1s, a1r, t, o).wait_send()

        @pl.when(t < ITERS - 1)
        def _():
            for o in range(1, N_ROW):
                along_row(b2, b2s, b2r, t, o).wait_send()
            for o in range(1, N_COL):
                along_col(b1, b1s, b1r, t, o).wait_send()

        return 0

    lax.fori_loop(0, ITERS, drain, 0)


def solve(table, weights, grads, x_blocks):
    vmem = lambda *shape, dtype=bf16: pltpu.VMEM(shape, dtype)
    sems = lambda *n: pltpu.SemaphoreType.DMA((ITERS, *n))
    half = (HALF, PIECE)
    shape = jax.ShapeDtypeStruct((N_ROW * PIECE, DIRS), f32)
    return pl.pallas_call(
        kernel,
        out_shape=(shape, shape),
        in_specs=[
            pl.BlockSpec(memory_space=pltpu.SMEM),
            pl.BlockSpec(memory_space=pltpu.VMEM),
            pl.BlockSpec(memory_space=pltpu.VMEM),
            pl.BlockSpec(memory_space=pl.ANY),
        ],
        out_specs=(pl.BlockSpec(memory_space=pltpu.VMEM), pl.BlockSpec(memory_space=pltpu.VMEM)),
        scratch_shapes=[
            vmem(NBLK + 1, BLK, BLK),
            vmem(NBLK + 1, BLK, BLK),
            vmem(2, N_ROW, *half, dtype=f32),
            vmem(2, N_ROW, *half, dtype=f32),
            vmem(2, N_ROW, *half, dtype=f32),
            vmem(2, N_ROW, *half),
            vmem(ITERS, 2, N_CHIP, *half),
            vmem(ITERS, 2, N_CHIP, *half),
            vmem(2, N_CHIP, *half, dtype=f32),
            vmem(ITERS, 2, N_CHIP, *half),
            vmem(ITERS, 2, N_CHIP, *half),
            vmem(2, *half, dtype=f32),
            vmem(ITERS, 2, N_COL, *half),
            vmem(2, N_ROW, *half, dtype=f32),
            vmem(ITERS, 2, N_ROW, *half),
            vmem(ITERS, 2, N_ROW, *half),
            vmem(ITERS, 2, N_ROW, *half),
            vmem(ITERS, N_COL, 8, DIRS, dtype=f32),
            vmem(ITERS, N_ROW, 8, DIRS, dtype=f32),
            vmem(ITERS, N_COL, 8, DIRS, dtype=f32),
            vmem(ITERS, N_ROW, 8, DIRS, dtype=f32),
            vmem(2, 2, HALF, BLK, dtype=f32),
            vmem(8, DIRS, dtype=f32),
            vmem(2, *half, dtype=f32),
            vmem(2, *half, dtype=f32),
            pltpu.SemaphoreType.DMA((8,)),
            *[sems(2, 8)] * 12,
            *[sems(16)] * 4,
            *[sems(8)] * 4,
        ],
        compiler_params=pltpu.CompilerParams(
            collective_id=0, has_side_effects=True, vmem_limit_bytes=60 * 2**20
        ),
    )(table, weights, grads, x_blocks)


def on_device(x_blocks, block_ids, margins, deleted, grads):
    ids = block_ids[:, 0]
    hit = jnp.arange(RB * FB, dtype=jnp.int32)[:, None] == ids[None, :]
    table = NBLK + jnp.sum(jnp.where(hit, jnp.arange(NBLK, dtype=jnp.int32)[None, :] - NBLK, 0), axis=1)
    r, c = lax.axis_index("row"), lax.axis_index("col")
    own = lax.dynamic_slice_in_dim(margins, c * PIECE, PIECE, 0)
    own_ids = r * margins.shape[0] + c * PIECE + jnp.arange(PIECE, dtype=jnp.int32)
    removed = jnp.any(own_ids[:, None] == deleted[None, :], axis=1)
    logistic = jax.nn.sigmoid(own)
    weights = jnp.where(removed, 0.0, logistic * (1.0 - logistic))[None, :]
    return solve(table, weights, grads, x_blocks)


def solution(mesh):
    in_specs = (P("row", "col", None), P("row", "col"), P("row"), P("row"), P("col", None))
    out_specs = (P("col", None), P("col", None))
    return jax.shard_map(on_device, mesh=mesh, in_specs=in_specs, out_specs=out_specs, check_vma=False)
```

time: 188 us -> 133 us (0.71)
  Pallas kernels: 178 us -> 123 us
    pallas_call x1, Pallas kernels: 178 us -> 123 us  [solve(): pl.pallas_call(kernel, out_shape=(shape, shape), in_specs=[pl.BlockSpec(m...]
where the time goes in v4:
time: 133 us; the launch traced here: 132 us
  Pallas kernels  123 us (92%)
  local copies, waits for them, and re-layouts  4.52 us (3%)
  other arithmetic  3.64 us (3%)
    pallas_call x1, Pallas kernels, solve(): pl.pallas_call(kernel, out_shape=(shape, shape), in_specs=[pl.BlockSpec(m...  123 us
    unnamed x2, local copies, waits for them, and re-layouts  4.52 us

profile of v4, /device:TPU:0, one launch (start us, length us, event | category | flops | bytes accessed | tf_op | source)
XLA Modules:
  0.0 132.1 jit_solution(9699948971568819449)
XLA Ops:
  0.6 0.9 compare_reduce_fusion
  1.5 1.3 %fusion = f32[256]{0:T(256)} fusion(pred[256]{0:T(512)(128)(4,1)S(1)} %compare_reduce_fusion, f32[4096]{0:T(1024)} %param.7, s32[]{:T(128)S(6)} %select_n.12), kind=kLoop, calls=%fused_computation.4 | loop fusion | flops 1536 | bytes 2308 | tf_op jit(solution)/shard_map/jit(_where)/select_n | solution.py:426
  2.9 0.8 select_reduce_fusion
  3.7 0.6 broadcast_add_fusion.table
  4.3 123.2 %shard_map.68 = (f32[2048,128]{1,0:T(8,128)}, f32[2048,128]{1,0:T(8,128)}) custom-call(s32[512]{0:T(512)} %broadcast_add_fusion.table, f32[1,256]{1,0:T(1,128)} %bitcast.2, f32[2048,128]{1,0:T(8,128)} %grads.1, bf16[256,128,128]{2,1,0:T(8,128)(2,1)} %x_hbm.1), custom_call_target="tpu_custom_call" | custom-call | tf_op jit(solution)/shard_map/pallas_call | solution.py:370
  127.5 2.3 %copy.9 = f32[2048,128]{1,0:T(8,128)} copy(f32[2048,128]{1,0:T(8,128)} %get-tuple-element.4) | data formatting | bytes 2097152
  129.8 2.3 %copy.10 = f32[2048,128]{1,0:T(8,128)} copy(f32[2048,128]{1,0:T(8,128)} %get-tuple-element.5) | data formatting | bytes 2097152
  (2 shorter events, 0.0 us)

commit v5 on v4

--- a/solution.py
+++ b/solution.py
@@ -9,6 +9,7 @@
 RIDGE = 0.2
 N_ROW, N_COL, N_CHIP = 8, 16, 8
 BLK, DIRS, FB, RB, NBLK = 128, 128, 16, 32, 256
+DELETED = 512
 PIECE = 256
 HALF = DIRS // 2
 WIDTH = 2
@@ -52,8 +53,8 @@
 
 
 def kernel(
-    table, weights, grads, x_hbm, out_sol, out_res,
-    x, xt, sol, res, d, v, psend, prec, pown, csend, crec, proj, s, acc, isend, irec, u,
+    table, margins, deleted, grads, x_hbm, sol, res,
+    x, xt, weights, d, v, psend, prec, pown, csend, crec, proj, s, acc, isend, irec, u,
     a1, a2, b1, b2, part, rr, alpha, beta,
     xsem, ps, pr, cs, cr, fs, fr, ss, sr, ims, imr, us, ur, a1s, a1r, b1s, b1r, a2s, a2r, b2s, b2r,
 ):
@@ -108,6 +109,14 @@
         return 0
 
     lax.fori_loop(0, N_ROW, begin, 0)
+    ids = lax.broadcasted_iota(jnp.int32, (BLK, PIECE), 1) + (r * N_COL + c) * PIECE
+    gone = jnp.zeros((BLK, PIECE), f32)
+    for i in range(DELETED // BLK):
+        listed = jnp.broadcast_to(deleted[:, i * BLK : (i + 1) * BLK].astype(f32), (BLK, BLK)).T
+        listed = jnp.concatenate([listed, listed], axis=1)
+        gone = jnp.where(listed == ids.astype(f32), 1.0, gone)
+    logistic = jax.nn.sigmoid(margins[:, pl.ds(pl.multiple_of(c * PIECE, PIECE), PIECE)])
+    weights[...] = jnp.where(jnp.max(gone, axis=0, keepdims=True) > 0.0, 0.0, logistic * (1.0 - logistic))
     for h in range(2):
         proj[h] = zero
         beta[h] = zero
@@ -177,6 +186,31 @@
             left = res[h, p] - alpha[h] * (u[t, h, p].astype(f32) + RIDGE * d[h, p])
             res[h, p] = left
             v[h, p] = left.astype(bf16)
+
+    def drain(t):
+        for h in range(2):
+            for o in range(N_CHIP):
+                to_sibling(t, h, o).wait_send()
+                across(t, h, o, c).wait_send()
+            for o in range(1, N_CHIP):
+                to_chip(t, h, o).wait_send()
+                direct(t, h, o, c).wait_send()
+                image(t, h, o).wait_send()
+        for o in range(1, N_ROW):
+            along_row(a2, a2s, a2r, t, o).wait_send()
+        for o in range(1, N_COL):
+            along_col(a1, a1s, a1r, t, o).wait_send()
+
+    def drain_updates(t):
+        for h in range(2):
+            for o in range(1, N_ROW):
+                update(t, h, o, r).wait_send()
+
+    def drain_beta(t):
+        for o in range(1, N_ROW):
+            along_row(b2, b2s, b2r, t, o).wait_send()
+        for o in range(1, N_COL):
+            along_col(b1, b1s, b1r, t, o).wait_send()
 
     def iteration(t, _):
         def forward(h, _):
@@ -319,69 +353,64 @@
             return 0
 
         lax.fori_loop(0, 2 * N_ROW, advance, 0, unroll=2)
+
+        @pl.when(t > 0)
+        def _():
+            drain_updates(t - 1)
+            drain_beta(t - 1)
+
+        drain(t)
         return 0
 
-    def write(state, out):
-        def turn_back(p, _):
-            both = jnp.concatenate([state[0, p], state[1, p]], axis=0)
-            out[pl.ds(pl.multiple_of(p * PIECE, PIECE), PIECE), :] = both.T
-            return 0
-
-        lax.fori_loop(0, N_ROW, turn_back, 0)
-
     lax.fori_loop(0, ITERS, iteration, 0)
-    write(sol, out_sol)
     for h in range(2):
         renew(ITERS - 1, h)
-    write(res, out_res)
-
-    def drain(t, _):
-        for h in range(2):
-            for o in range(N_CHIP):
-                to_sibling(t, h, o).wait_send()
-                across(t, h, o, c).wait_send()
-            for o in range(1, N_CHIP):
-                to_chip(t, h, o).wait_send()
-                direct(t, h, o, c).wait_send()
-                image(t, h, o).wait_send()
-                update(t, h, o, r).wait_send()
-        for o in range(1, N_ROW):
-            along_row(a2, a2s, a2r, t, o).wait_send()
-        for o in range(1, N_COL):
-            along_col(a1, a1s, a1r, t, o).wait_send()
-
-        @pl.when(t < ITERS - 1)
-        def _():
-            for o in range(1, N_ROW):
-                along_row(b2, b2s, b2r, t, o).wait_send()
-            for o in range(1, N_COL):
-                along_col(b1, b1s, b1r, t, o).wait_send()
-
-        return 0
-
-    lax.fori_loop(0, ITERS, drain, 0)
-
-
-def solve(table, weights, grads, x_blocks):
+
+    drain_updates(ITERS - 1)
+
+
+def turn_back(sol, res, out_sol, out_res):
+    for state, out in ((sol, out_sol), (res, out_res)):
+        for p in range(state.shape[1]):
+            out[p * PIECE : (p + 1) * PIECE, :] = jnp.concatenate([state[0, p], state[1, p]], axis=0).T
+
+
+def turned_back(sol, res):
+    shape = jax.ShapeDtypeStruct((N_ROW * PIECE, DIRS), f32)
+    steps = 4
+    each = N_ROW // steps
+    taken = pl.BlockSpec((2, each, HALF, PIECE), lambda i: (0, i, 0, 0))
+    given = pl.BlockSpec((each * PIECE, DIRS), lambda i: (i, 0))
+    return pl.pallas_call(
+        turn_back,
+        out_shape=(shape, shape),
+        grid=(steps,),
+        in_specs=[taken, taken],
+        out_specs=(given, given),
+    )(sol, res)
+
+
+def solve(table, margins, deleted, grads, x_blocks):
     vmem = lambda *shape, dtype=bf16: pltpu.VMEM(shape, dtype)
     sems = lambda *n: pltpu.SemaphoreType.DMA((ITERS, *n))
     half = (HALF, PIECE)
-    shape = jax.ShapeDtypeStruct((N_ROW * PIECE, DIRS), f32)
+    shape = jax.ShapeDtypeStruct((2, N_ROW, *half), f32)
+    in_vmem = pl.BlockSpec(memory_space=pltpu.VMEM)
     return pl.pallas_call(
         kernel,
         out_shape=(shape, shape),
         in_specs=[
             pl.BlockSpec(memory_space=pltpu.SMEM),
-            pl.BlockSpec(memory_space=pltpu.VMEM),
-            pl.BlockSpec(memory_space=pltpu.VMEM),
+            in_vmem,
+            in_vmem,
+            in_vmem,
             pl.BlockSpec(memory_space=pl.ANY),
         ],
-        out_specs=(pl.BlockSpec(memory_space=pltpu.VMEM), pl.BlockSpec(memory_space=pltpu.VMEM)),
+        out_specs=(in_vmem, in_vmem),
         scratch_shapes=[
             vmem(NBLK + 1, BLK, BLK),
             vmem(NBLK + 1, BLK, BLK),
-            vmem(2, N_ROW, *half, dtype=f32),
-            vmem(2, N_ROW, *half, dtype=f32),
+            vmem(1, PIECE, dtype=f32),
             vmem(2, N_ROW, *half, dtype=f32),
             vmem(2, N_ROW, *half),
             vmem(ITERS, 2, N_CHIP, *half),
@@ -411,20 +440,13 @@
         compiler_params=pltpu.CompilerParams(
             collective_id=0, has_side_effects=True, vmem_limit_bytes=60 * 2**20
         ),
-    )(table, weights, grads, x_blocks)
+    )(table, margins, deleted, grads, x_blocks)
 
 
 def on_device(x_blocks, block_ids, margins, deleted, grads):
-    ids = block_ids[:, 0]
-    hit = jnp.arange(RB * FB, dtype=jnp.int32)[:, None] == ids[None, :]
-    table = NBLK + jnp.sum(jnp.where(hit, jnp.arange(NBLK, dtype=jnp.int32)[None, :] - NBLK, 0), axis=1)
-    r, c = lax.axis_index("row"), lax.axis_index("col")
-    own = lax.dynamic_slice_in_dim(margins, c * PIECE, PIECE, 0)
-    own_ids = r * margins.shape[0] + c * PIECE + jnp.arange(PIECE, dtype=jnp.int32)
-    removed = jnp.any(own_ids[:, None] == deleted[None, :], axis=1)
-    logistic = jax.nn.sigmoid(own)
-    weights = jnp.where(removed, 0.0, logistic * (1.0 - logistic))[None, :]
-    return solve(table, weights, grads, x_blocks)
+    hit = jnp.arange(RB * FB, dtype=jnp.int32)[:, None] == block_ids[:, 0][None, :]
+    table = jnp.min(jnp.where(hit, jnp.arange(NBLK, dtype=jnp.int32)[None, :], NBLK), axis=1)
+    return turned_back(*solve(table, margins[None, :], deleted[None, :], grads, x_blocks))
 
 
 def solution(mesh):

time: 133 us -> 129 us (0.970)
  local copies, waits for them, and re-layouts: 4.52 us -> 0 us
  Pallas kernels: 123 us -> 126 us
  other arithmetic: 3.64 us -> 1.41 us
    unnamed x2 -> x0, local copies, waits for them, and re-layouts: 4.52 us -> none
    pallas_call x0 -> x1, Pallas kernels: none -> 3.96 us  [turned_back(): pl.pallas_call(turn_back, out_shape=(shape, shape), grid=(steps,), in_spe...]
    reduce_min x0 -> x1, other arithmetic: none -> 1.41 us  [on_device(): jnp.min(jnp.where(hit, jnp.arange(NBLK, dtype=jnp.int32)[None, :], NBLK),...]
    select_n x1 -> x0, other arithmetic: 1.34 us -> none  [on_device(): weights = jnp.where(removed, 0.0, logistic * (1.0 - logistic))[None, :]]
where the time goes in v5:
time: 129 us; the launch traced here: 128 us
  Pallas kernels  126 us (98%)
  other arithmetic  1.41 us (1%)
    pallas_call x1, Pallas kernels, solve(): pl.pallas_call(kernel, out_shape=(shape, shape), in_specs=[pl.BlockSpec(m...  122 us
    pallas_call x1, Pallas kernels, turned_back(): pl.pallas_call(turn_back, out_shape=(shape, shape), grid=(steps,), in_spe...  3.96 us

profile of v5, /device:TPU:0, one launch (start us, length us, event | category | flops | bytes accessed | tf_op | source)
XLA Modules:
  0.0 128.2 jit_solution(6409392403663124990)
XLA Ops:
  0.6 1.4 %select_reduce_fusion.table = s32[512]{0:T(512)} fusion(s32[256]{0:T(256)} %bitcast.5), kind=kLoop, calls=%fused_computation | loop fusion | flops 392704 | bytes 3072 | tf_op jit(solution)/shard_map/reduce_min | solution.py:448
  2.0 122.2 %shard_map.68 = (f32[2,8,64,256]{3,2,1,0:T(8,128)}, f32[2,8,64,256]{3,2,1,0:T(8,128)}) custom-call(s32[512]{0:T(512)} %select_reduce_fusion.table, f32[1,4096]{1,0:T(1,128)} %bitcast.3, s32[1,512]{1,0:T(1,128)} %bitcast.4, f32[2048,128]{1,0:T(8,128)} %grads.1, bf16[256,128,128]{2,1,0:T(8,128)(2,1)} %x_hbm.1), custom_call_target="tpu_custom_call" | custom-call | tf_op jit(solution)/shard_map/pallas_call | solution.py:399
  124.2 4.0 %shard_map.69 = (f32[2048,128]{1,0:T(8,128)}, f32[2048,128]{1,0:T(8,128)}) custom-call(f32[2,8,64,256]{3,2,1,0:T(8,128)} %get-tuple-element.4.sol, f32[2,8,64,256]{3,2,1,0:T(8,128)} %get-tuple-element.5.res), custom_call_target="tpu_custom_call" | custom-call | tf_op jit(solution)/shard_map/pallas_call | solution.py:384

commit v6 on v5

--- a/solution.py
+++ b/solution.py
@@ -13,6 +13,8 @@
 PIECE = 256
 HALF = DIRS // 2
 WIDTH = 2
+STEPS = 2
+CUTS = (0, 3, 6, 8)
 CHIP_ORDER = (5, 1, 3, 7, 4, 2, 6)
 ROW_ORDER = (6, 2, 5, 7, 4, 1, 3)
 f32, bf16 = jnp.float32, jnp.bfloat16
@@ -53,8 +55,8 @@
 
 
 def kernel(
-    table, margins, deleted, grads, x_hbm, sol, res,
-    x, xt, weights, d, v, psend, prec, pown, csend, crec, proj, s, acc, isend, irec, u,
+    table, margins, deleted, grads, x_hbm, out_sol, res,
+    x, xt, weights, sol, d, v, psend, prec, pown, csend, crec, proj, s, acc, isend, irec, u,
     a1, a2, b1, b2, part, rr, alpha, beta,
     xsem, ps, pr, cs, cr, fs, fr, ss, sr, ims, imr, us, ur, a1s, a1r, b1s, b1r, a2s, a2r, b2s, b2r,
 ):
@@ -283,19 +285,21 @@
             order = (0, *CHIP_ORDER)
 
             def stage(g):
-                for o in order[2 * g : 2 * g + 2]:
+                for o in order[CUTS[g] : CUTS[g + 1]]:
                     if o > 0:
                         j = chip_from(o) * 2 + k
                         direct(t, h, o, j).wait_recv()
                         across(t, h, o, j).start()
 
+            last = len(CUTS) - 2
             stage(0)
-            for g in range(4):
-                if g < 3:
+            for g in range(last + 1):
+                if g < last:
                     stage(g + 1)
-                for o in order[2 * g : 2 * g + 2]:
+                group = order[CUTS[g] : CUTS[g + 1]]
+                for o in group:
                     across(t, h, o, chip_from(o) * 2 + 1 - k).wait_recv()
-                js = [chip_from(o) * 2 + kk for o in order[2 * g : 2 * g + 2] for kk in (0, 1)]
+                js = [chip_from(o) * 2 + kk for o in group for kk in (0, 1)]
                 outs = []
                 rows = (*ROW_ORDER, 0)
                 for o in rows:
@@ -307,7 +311,7 @@
                 for o, out in zip(rows, outs):
                     if g > 0:
                         out += acc[h, o]
-                    if g < 3 or o == 0:
+                    if g < last or o == 0:
                         acc[h, o] = out
                     else:
                         isend[t, h, o] = out.astype(bf16)
@@ -359,6 +363,15 @@
             drain_updates(t - 1)
             drain_beta(t - 1)
 
+        @pl.when(t == ITERS - 1)
+        def _():
+            def turn(p, _):
+                both = jnp.concatenate([sol[0, p], sol[1, p]], axis=0)
+                out_sol[pl.ds(pl.multiple_of(p * PIECE, PIECE), PIECE), :] = both.T
+                return 0
+
+            lax.fori_loop(0, N_ROW, turn, 0)
+
         drain(t)
         return 0
 
@@ -370,14 +383,14 @@
 
 
 def turn_back(sol, res, out_sol, out_res):
-    for state, out in ((sol, out_sol), (res, out_res)):
-        for p in range(state.shape[1]):
-            out[p * PIECE : (p + 1) * PIECE, :] = jnp.concatenate([state[0, p], state[1, p]], axis=0).T
+    out_sol[...] = sol[...]
+    for p in range(res.shape[1]):
+        out_res[p * PIECE : (p + 1) * PIECE, :] = jnp.concatenate([res[0, p], res[1, p]], axis=0).T
 
 
 def turned_back(sol, res):
     shape = jax.ShapeDtypeStruct((N_ROW * PIECE, DIRS), f32)
-    steps = 4
+    steps = STEPS
     each = N_ROW // steps
     taken = pl.BlockSpec((2, each, HALF, PIECE), lambda i: (0, i, 0, 0))
     given = pl.BlockSpec((each * PIECE, DIRS), lambda i: (i, 0))
@@ -385,7 +398,7 @@
         turn_back,
         out_shape=(shape, shape),
         grid=(steps,),
-        in_specs=[taken, taken],
+        in_specs=[given, taken],
         out_specs=(given, given),
     )(sol, res)
 
@@ -395,10 +408,11 @@
     sems = lambda *n: pltpu.SemaphoreType.DMA((ITERS, *n))
     half = (HALF, PIECE)
     shape = jax.ShapeDtypeStruct((2, N_ROW, *half), f32)
+    rows = jax.ShapeDtypeStruct((N_ROW * PIECE, DIRS), f32)
     in_vmem = pl.BlockSpec(memory_space=pltpu.VMEM)
     return pl.pallas_call(
         kernel,
-        out_shape=(shape, shape),
+        out_shape=(rows, shape),
         in_specs=[
             pl.BlockSpec(memory_space=pltpu.SMEM),
             in_vmem,
@@ -411,6 +425,7 @@
             vmem(NBLK + 1, BLK, BLK),
             vmem(NBLK + 1, BLK, BLK),
             vmem(1, PIECE, dtype=f32),
+            vmem(2, N_ROW, *half, dtype=f32),
             vmem(2, N_ROW, *half, dtype=f32),
             vmem(2, N_ROW, *half),
             vmem(ITERS, 2, N_CHIP, *half),

time: 129 us -> 126 us (0.977)
  Pallas kernels: 126 us -> 124 us
    pallas_call x1, Pallas kernels: 122 us -> 121 us  [solve(): pl.pallas_call(kernel, out_shape=(rows, shape), in_specs=[pl.BlockSpec(me...]
where the time goes in v6:
time: 126 us
  Pallas kernels  124 us (98%)
  other arithmetic  1.41 us (1%)
    pallas_call x1, Pallas kernels, solve(): pl.pallas_call(kernel, out_shape=(rows, shape), in_specs=[pl.BlockSpec(me...  121 us
    pallas_call x1, Pallas kernels, turned_back(): pl.pallas_call(turn_back, out_shape=(shape, shape), grid=(steps,), in_spe...  2.67 us

profile of v6, /device:TPU:0, one launch (start us, length us, event | category | flops | bytes accessed | tf_op | source)
XLA Modules:
  0.0 125.6 jit_solution(743453173924621877)
XLA Ops:
  0.6 1.4 %select_reduce_fusion.table = s32[512]{0:T(512)} fusion(s32[256]{0:T(256)} %bitcast.5), kind=kLoop, calls=%fused_computation | loop fusion | flops 392704 | bytes 3072 | tf_op jit(solution)/shard_map/reduce_min | solution.py:463
  2.0 120.9 %shard_map.68 = (f32[2048,128]{1,0:T(8,128)}, f32[2,8,64,256]{3,2,1,0:T(8,128)}) custom-call(s32[512]{0:T(512)} %select_reduce_fusion.table, f32[1,4096]{1,0:T(1,128)} %bitcast.3, s32[1,512]{1,0:T(1,128)} %bitcast.4, f32[2048,128]{1,0:T(8,128)} %grads.1, bf16[256,128,128]{2,1,0:T(8,128)(2,1)} %x_hbm.1), custom_call_target="tpu_custom_call" | custom-call | tf_op jit(solution)/shard_map/pallas_call | solution.py:413
  122.9 2.7 %shard_map.69 = (f32[2048,128]{1,0:T(8,128)}, f32[2048,128]{1,0:T(8,128)}) custom-call(f32[2048,128]{1,0:T(8,128)} %get-tuple-element.4.sol, f32[2,8,64,256]{3,2,1,0:T(8,128)} %get-tuple-element.5.res), custom_call_target="tpu_custom_call" | custom-call | tf_op jit(solution)/shard_map/pallas_call | solution.py:397

commit v7 on v6

--- a/solution.py
+++ b/solution.py
@@ -13,7 +13,7 @@
 PIECE = 256
 HALF = DIRS // 2
 WIDTH = 2
-STEPS = 2
+STEPS = 1
 CUTS = (0, 3, 6, 8)
 CHIP_ORDER = (5, 1, 3, 7, 4, 2, 6)
 ROW_ORDER = (6, 2, 5, 7, 4, 1, 3)

time: 126 us -> 126 us (level)
  no operation moved by 1% of the time
where the time goes in v7:
time: 126 us
  Pallas kernels  124 us (98%)
  other arithmetic  1.41 us (1%)
    pallas_call x1, Pallas kernels, solve(): pl.pallas_call(kernel, out_shape=(rows, shape), in_specs=[pl.BlockSpec(me...  121 us
    pallas_call x1, Pallas kernels, turned_back(): pl.pallas_call(turn_back, out_shape=(shape, shape), grid=(steps,), in_spe...  3.18 us

profile of v7, /device:TPU:0, one launch (start us, length us, event | category | flops | bytes accessed | tf_op | source)
XLA Modules:
  0.0 126.1 jit_solution(5098480708774491688)
XLA Ops:
  0.6 1.4 %select_reduce_fusion.table = s32[512]{0:T(512)} fusion(s32[256]{0:T(256)} %bitcast.5), kind=kLoop, calls=%fused_computation | loop fusion | flops 392704 | bytes 3072 | tf_op jit(solution)/shard_map/reduce_min | solution.py:463
  2.0 120.9 %shard_map.68 = (f32[2048,128]{1,0:T(8,128)}, f32[2,8,64,256]{3,2,1,0:T(8,128)}) custom-call(s32[512]{0:T(512)} %select_reduce_fusion.table, f32[1,4096]{1,0:T(1,128)} %bitcast.3, s32[1,512]{1,0:T(1,128)} %bitcast.4, f32[2048,128]{1,0:T(8,128)} %grads.1, bf16[256,128,128]{2,1,0:T(8,128)(2,1)} %x_hbm.1), custom_call_target="tpu_custom_call" | custom-call | tf_op jit(solution)/shard_map/pallas_call | solution.py:413
  122.9 3.2 %shard_map.69 = (f32[2048,128]{1,0:T(8,128)}, f32[2048,128]{1,0:T(8,128)}) custom-call(f32[2048,128]{1,0:T(8,128)} %get-tuple-element.4.sol, f32[2,8,64,256]{3,2,1,0:T(8,128)} %get-tuple-element.5.res), custom_call_target="tpu_custom_call" | custom-call | tf_op jit(solution)/shard_map/pallas_call | solution.py:397
